TPU v7x, 128 devices: a whole 4x4x4 slice. The times are simulated.
128 devices in a mesh: ctx: 16 (over x, y), head: 8 (over z, core).
Axes of the slice: x: 4, y: 4, z: 4, core: 2. Of those that a mesh axis runs over, the one named last changes fastest.
Arguments:
- queries: bfloat16 [10240, 32, 128], P('ctx', 'head'), may hold values from -8 to 8
- key_rows: bfloat16 [10240, 32, 128], P('ctx', 'head'), may hold values from -8 to 8
- value_rows: bfloat16 [10240, 32, 128], P('ctx', 'head'), may hold values from -6 to 6
- out_weight: bfloat16 [32, 128, 4096], P('head'), may hold values from -0.09375 to 0.09375
- out_grad: bfloat16 [10240, 4096], P('ctx', 'head'), may hold values from -6 to 6
- global_ids: int32 [2], replicated, may hold values from 0 to 159, as said below
- random_ids: int32 [160, 3], replicated, may hold values from 0 to 159, as said below
- random_count: int32 [160], replicated, may hold values from 1 to 3
Outputs:
- projected: bfloat16 [10240, 4096], P('ctx', 'head')
- query_grad: bfloat16 [10240, 32, 128], P('ctx', 'head')
- key_grad: bfloat16 [10240, 32, 128], P('ctx', 'head')
- value_grad: bfloat16 [10240, 32, 128], P('ctx', 'head')
Inputs may be any that keep to these rules, and one draw needn't show every extreme that they name: `global_ids`: 2 distinct block numbers; the last block is one of them. `random_ids`: block numbers; padded slots hold block numbers too. The 30 entries of the query blocks of one index of ctx (blocks k * 10 to k * 10 + 9) name blocks held by any one index at most 3 times, and in every draw some index is named exactly 3 times by the entries of every index.
All inputs are finite; a program needn't handle non-finite values.
Results may differ from a plain program's by a relative error of at most 0.03.
Values may be sent and summed in bfloat16 or wider, within the bound.
A program may use at most 192 MiB of HBM per device.

v0:
```python
import math

import jax
import jax.numpy as jnp
from jax import lax
from jax.sharding import PartitionSpec as P

BLOCK = 64
G = 2
R = 3


def with_halo(x, sides, width):
    for axis, dim in sides:
        count, length = (lax.axis_size(axis), x.shape[dim])
        up = [(i, (i + 1) % count) for i in range(count - 1)]
        down = [(j, i) for i, j in up]
        last = lax.slice_in_dim(x, length - width, length, axis=dim)
        first = lax.slice_in_dim(x, 0, width, axis=dim)
        before = lax.ppermute(last, axis, up)
        after = lax.ppermute(first, axis, down)
        x = jnp.concatenate([before, x, after], axis=dim)
    return x


def local(
    queries, key_rows, value_rows, out_weight, out_grad, global_ids, random_ids, random_count
):
    tok_rows, heads_here, head_dim = queries.shape
    blocks_here = tok_rows // BLOCK
    shards = lax.axis_size("ctx")
    blocks_all = blocks_here * shards
    my_index = lax.axis_index("ctx")
    first_block = my_index * blocks_here
    score_scale = 1.0 / math.sqrt(head_dim)
    capacity = max(2, (4 * blocks_here * R + 3 * shards - 1) // (3 * shards))
    slot_total = blocks_here * R
    tail_shape = (BLOCK, heads_here, head_dim)
    stacked = jnp.stack([key_rows, value_rows], axis=0)
    rimmed = with_halo(stacked, (("ctx", 1),), BLOCK)
    rim_blocks = rimmed.reshape((2, blocks_here + 2) + tail_shape)
    window = jnp.stack(
        [
            rim_blocks[:, 0:blocks_here],
            rim_blocks[:, 1 : blocks_here + 1],
            rim_blocks[:, 2 : blocks_here + 2],
        ],
        axis=2,
    )
    mine_ids = lax.dynamic_slice_in_dim(random_ids, first_block, blocks_here, 0).reshape(slot_total)
    owners = mine_ids // blocks_here
    same_owner = owners[:, None] == owners[None, :]
    earlier = (
        jnp.arange(slot_total, dtype=jnp.int32)[None, :]
        < jnp.arange(slot_total, dtype=jnp.int32)[:, None]
    )
    owner_rank = jnp.sum((same_owner & earlier).astype(jnp.int32), axis=1)
    slot_index = owners * capacity + owner_rank
    all_requests = random_ids.reshape(shards, slot_total)
    asked_owner = all_requests // blocks_here
    asked_local = all_requests - asked_owner * blocks_here
    asked_mine = asked_owner == my_index
    order_rank = jnp.cumsum(asked_mine.astype(jnp.int32), axis=1) - 1
    slot_hits = asked_mine[:, :, None] & (
        order_rank[:, :, None] == jnp.arange(capacity, dtype=jnp.int32)[None, None, :]
    )
    send_local = jnp.sum(jnp.where(slot_hits, asked_local[:, :, None], 0), axis=1)
    send_used = jnp.any(slot_hits, axis=1)
    glob_owner = global_ids // blocks_here
    glob_local = global_ids - glob_owner * blocks_here
    everything = lax.all_gather(stacked, "ctx", axis=1, tiled=True)
    all_blocks = everything.reshape((2, blocks_all) + tail_shape)
    global_blocks = all_blocks[:, global_ids]
    randoms = all_blocks[:, mine_ids]
    global_each = jnp.broadcast_to(global_blocks[:, None], (2, blocks_here, G) + tail_shape)
    random_each = randoms.reshape((2, blocks_here, R) + tail_shape)
    listed = jnp.concatenate([window, global_each, random_each], axis=2)
    listed = jnp.transpose(listed, (0, 1, 4, 2, 3, 5))
    key_list = listed[0]
    value_list = listed[1]
    block_global = first_block + jnp.arange(blocks_here, dtype=jnp.int32)
    left_ok = block_global > 0
    right_ok = block_global < blocks_all - 1
    counts_here = lax.dynamic_slice_in_dim(random_count, first_block, blocks_here, 0)
    keep_mask = jnp.concatenate(
        [
            left_ok[:, None],
            jnp.ones((blocks_here, 1), dtype=bool),
            right_ok[:, None],
            jnp.ones((blocks_here, G), dtype=bool),
            jnp.arange(R, dtype=jnp.int32)[None, :] < counts_here[:, None],
        ],
        axis=1,
    )
    q_blocks = jnp.transpose(queries.reshape((blocks_here,) + tail_shape), (0, 2, 1, 3))
    scores = (
        jnp.einsum("jhqd,jhskd->jhqsk", q_blocks, key_list, preferred_element_type=jnp.float32)
        * score_scale
    )
    scores = jnp.where(keep_mask[:, None, None, :, None], scores, -jnp.inf)
    row_peak = jnp.max(scores, axis=(3, 4), keepdims=True)
    weights_raw = jnp.exp(scores - row_peak)
    probabilities = weights_raw / jnp.sum(weights_raw, axis=(3, 4), keepdims=True)
    probs_low = probabilities.astype(jnp.bfloat16)
    attended = jnp.einsum(
        "jhqsk,jhskd->jhqd", probs_low, value_list, preferred_element_type=jnp.float32
    ).astype(jnp.bfloat16)
    attended_rows = jnp.transpose(attended, (0, 2, 1, 3)).reshape(tok_rows, heads_here * head_dim)
    weight_flat = out_weight.reshape(heads_here * head_dim, out_weight.shape[2])
    partial_out = jnp.dot(attended_rows, weight_flat, preferred_element_type=jnp.float32)
    projected = lax.psum_scatter(partial_out, "head", scatter_dimension=1, tiled=True).astype(
        jnp.bfloat16
    )
    grad_total = lax.dot_general(
        lax.all_gather(out_grad, "head", axis=1, tiled=True),
        weight_flat,
        (((1,), (1,)), ((), ())),
        preferred_element_type=jnp.float32,
    )
    attended_grad = jnp.transpose(
        grad_total.astype(jnp.bfloat16).reshape((blocks_here,) + tail_shape), (0, 2, 1, 3)
    )
    row_delta = jnp.sum(attended_grad.astype(jnp.float32) * attended.astype(jnp.float32), axis=3)
    prob_grad = jnp.einsum(
        "jhqd,jhskd->jhqsk", attended_grad, value_list, preferred_element_type=jnp.float32
    )
    score_grad = (probabilities * (prob_grad - row_delta[:, :, :, None, None])).astype(jnp.bfloat16)
    query_heads = (
        jnp.einsum("jhqsk,jhskd->jhqd", score_grad, key_list, preferred_element_type=jnp.float32)
        * score_scale
    ).astype(jnp.bfloat16)
    query_grad = jnp.transpose(query_heads, (0, 2, 1, 3)).reshape(tok_rows, heads_here, head_dim)
    key_part = (
        jnp.einsum("jhqsk,jhqd->jhskd", score_grad, q_blocks, preferred_element_type=jnp.float32)
        * score_scale
    )
    value_part = jnp.einsum(
        "jhqsk,jhqd->jhskd", probs_low, attended_grad, preferred_element_type=jnp.float32
    )
    pair_parts = jnp.transpose(jnp.stack([key_part, value_part], axis=0), (0, 1, 3, 4, 2, 5))
    zero_block = jnp.zeros((2, 1) + tail_shape, jnp.float32)
    summed = jnp.concatenate([zero_block, pair_parts[:, :, 1], zero_block], axis=1)
    summed = summed + jnp.concatenate([pair_parts[:, :, 0], zero_block, zero_block], axis=1)
    summed = summed + jnp.concatenate([zero_block, zero_block, pair_parts[:, :, 2]], axis=1)
    edge_rows = jnp.concatenate([summed[:, 0], summed[:, blocks_here + 1]], axis=1)
    rimmed_grads = with_halo(edge_rows.astype(jnp.bfloat16), (("ctx", 1),), BLOCK).astype(
        edge_rows.dtype
    )
    own_blocks = summed[:, 1 : blocks_here + 1]
    own_blocks = own_blocks.at[:, 0].add(rimmed_grads[:, 0:BLOCK])
    own_blocks = own_blocks.at[:, blocks_here - 1].add(rimmed_grads[:, 3 * BLOCK : 4 * BLOCK])
    global_sums = jnp.sum(pair_parts[:, :, 3 : 3 + G], axis=1)
    global_total = lax.psum(global_sums.astype(jnp.bfloat16), "ctx").astype(jnp.float32)
    global_place = (
        (glob_local[:, None] == jnp.arange(blocks_here, dtype=jnp.int32)[None, :])
        & (glob_owner == my_index)[:, None]
    ).astype(jnp.float32)
    own_blocks = own_blocks + jnp.einsum(
        "gb,xgkhd->xbkhd", global_place, global_total, precision=lax.Precision.HIGHEST
    )
    random_parts = (
        pair_parts[:, :, 3 + G :].astype(jnp.bfloat16).reshape((2, slot_total) + tail_shape)
    )
    back_buffer = (
        jnp.zeros((2, shards * capacity) + tail_shape, jnp.bfloat16)
        .at[:, slot_index]
        .set(random_parts)
    )
    returned = lax.all_to_all(
        back_buffer.reshape((2, shards, capacity) + tail_shape),
        "ctx",
        split_axis=1,
        concat_axis=1,
        tiled=True,
    )
    random_place = (
        (send_local.reshape(-1)[:, None] == jnp.arange(blocks_here, dtype=jnp.int32)[None, :])
        & send_used.reshape(-1)[:, None]
    ).astype(jnp.bfloat16)
    own_blocks = own_blocks + jnp.einsum(
        "mb,xmkhd->xbkhd",
        random_place,
        returned.reshape((2, shards * capacity) + tail_shape),
        preferred_element_type=jnp.float32,
    )
    key_grad = own_blocks[0].reshape(tok_rows, heads_here, head_dim).astype(jnp.bfloat16)
    value_grad = own_blocks[1].reshape(tok_rows, heads_here, head_dim).astype(jnp.bfloat16)
    return (projected, query_grad, key_grad, value_grad)


def solution(mesh):
    placed = (
        P("ctx", "head", None),
        P("ctx", "head", None),
        P("ctx", "head", None),
        P("head", None, None),
        P("ctx", "head"),
        P(),
        P(),
        P(),
    )
    return jax.shard_map(
        local,
        mesh=mesh,
        in_specs=placed,
        out_specs=(
            P("ctx", "head"),
            P("ctx", "head", None),
            P("ctx", "head", None),
            P("ctx", "head", None),
        ),
        check_vma=False,
    )
```

profile of v0, /device:TPU:1, one launch (start us, length us, event | category | flops | bytes accessed | tf_op | source)
XLA Modules:
  0.0 496.5 jit_solution(14105523715873079521)
XLA Ops:
  8.0 1.5 copy_bitcast_fusion.3
  10.8 4.0 collective-permute-start
  14.8 1.3 collective-permute-start.1
  17.3 3.2 collective-permute-done.1
  21.7 1.5 fusion.24
  23.2 1.4 fusion.23
  24.6 1.4 fusion.22
  26.0 24.1 %all-gather.5.cloned.1.call-done = bf16[640,4096]{1,0:T(8,128)(2,1)} async-done(((bf16[640,512]{1,0:T(8,128)(2,1)}), bf16[640,4096]{1,0:T(8,128)(2,1)}) %all-gather.5.cloned.1.call-update) | async-done | bytes 5242896 | tf_op jit(solution)/shard_map/all_gather | solution.py:115
  50.1 6.7 %convolution_convert_fusion = bf16[640,512]{1,0:T(8,128)(2,1)S(1)} fusion(bf16[640,4096]{1,0:T(8,128)(2,1)} %all-gather.5.cloned.1.call-done, bf16[512,4096]{1,0:T(8,128)(2,1)} %bitcast.200), kind=kOutput, calls=%fused_computation.45 | convolution fusion | flops 2684682240 | bytes 10092544 | tf_op jit(solution)/shard_map/dot_general | solution.py:114
  56.9 127.4 %all-gather.3.cloned.1.call-done = bf16[2,10240,4,128]{3,1,2,0:T(8,128)(2,1)} async-done(((bf16[2,640,4,128]{3,1,2,0:T(8,128)(2,1)}), bf16[2,10240,4,128]{3,1,2,0:T(8,128)(2,1)}) %all-gather.3.cloned.1.call-update) | async-done | bytes 20971536 | tf_op jit(solution)/shard_map/all_gather | solution.py:71
  184.3 17.5 %copy.142 = bf16[2,160,64,4,128]{4,2,3,1,0:T(8,128)(2,1)} copy(bf16[2,160,64,4,128]{4,2,1,3,0:T(8,128)(2,1)} %bitcast.192) | data formatting | bytes 41943040 | tf_op jit(solution)/shard_map/reshape | solution.py:72
  201.9 9.9 %gather_fusion.1 = bf16[30,2,64,4,128]{4,2,3,1,0:T(8,128)(2,1)} fusion(bf16[2,160,64,4,128]{4,2,1,3,0:T(8,128)(2,1)} %bitcast.193, s32[1024]{0:T(1024)S(1)} %get-tuple-element.73), kind=kCustom, calls=%fused_computation.1 | custom fusion | bytes 7864440 | tf_op jit(solution)/shard_map/gather | solution.py:74
  211.8 7.6 %gather_fusion = bf16[2,2,64,4,128]{4,2,3,1,0:T(8,128)(2,1)S(1)} fusion(bf16[2,160,64,4,128]{4,2,3,1,0:T(8,128)(2,1)} %copy.142, s32[1024]{0:T(1024)S(1)} %get-tuple-element.74), kind=kCustom, calls=%fused_computation | custom fusion | bytes 524296 | tf_op jit(solution)/shard_map/gather | solution.py:73
  219.4 2.2 broadcast_dynamic-update-slice_fusion
  221.6 5.3 %copy_dynamic-update-slice_fusion = bf16[2,10,8,64,4,128]{5,3,2,4,1,0:T(8,128)(2,1)} fusion(bf16[2,10,8,64,4,128]{5,3,2,4,1,0:T(8,128)(2,1)} %broadcast_dynamic-update-slice_fusion, bf16[2,10,3,64,4,128]{5,3,4,0,2,1:T(8,128)(2,1)} %bitcast.196), kind=kLoop, calls=%fused_computation.22 | loop fusion | bytes 7864320 | tf_op jit(solution)/shard_map/concatenate | solution.py:77
  226.9 4.1 bitcast_reduce_fusion
  231.0 3.9 copy-done.3
  234.9 3.0 fusion.2
  237.9 8.8 %multiply_reduce_fusion = (f32[10,4,64]{2,1,0:T(4,128)S(1)}, bf16[10,4,64,128]{3,2,1,0:T(8,128)(2,1)S(1)}) fusion(bf16[10,64,4,128]{3,2,1,0:T(4,128)(2,1)S(1)} %reshape.344, bf16[2,10,4,8,64,128]{5,4,3,2,1,0:T(8,128)(2,1)} %bitcast.11, f32[10,4,64]{2,1,0:T(4,128)S(1)} %fusion.2, f32[10,4,64]{2,1,0:T(4,128)S(1)} %get-tuple-element.67, ...), kind=kOutput, calls=%fused_computation.52 | convolution fusion | flops 343733760 | bytes 17070160 | tf_op jit(solution)/shard_map/jhqsk,jhskd->jhqd/dot_general | solution.py:105
  246.7 10.3 %convolution_bitcast_fusion = f32[1,10,4,8,64,128]{5,4,3,2,1,0:T(8,128)} fusion(bf16[10,64,4,128]{3,2,1,0:T(4,128)(2,1)S(1)} %reshape.344, f32[10,4,8,64,64]{4,3,2,1,0:T(8,128)} %copy-done.3, f32[10,4,64]{2,1,0:T(4,128)S(1)} %fusion.2, f32[10,4,64]{2,1,0:T(4,128)S(1)} %get-tuple-element.67, pred[10,8]{1,0:T(8,128)(4,1)S(1)} %concatenate.28), kind=kOutput, calls=%fused_computation.23 | convolution fusion | flops 342097920 | bytes 16404560 | tf_op jit(solution)/shard_map/jhqsk,jhqd->jhskd/dot_general | solution.py:137
  257.5 7.6 %multiply_convert_fusion = bf16[10,4,64,8,64]{2,4,3,1,0:T(8,128)(2,1)S(1)} fusion(f32[10,4,64]{2,1,0:T(4,128)S(1)} %get-tuple-element.69, bf16[2,10,4,8,64,128]{5,4,3,2,1,0:T(8,128)(2,1)} %bitcast.11, bf16[10,64,4,128]{3,2,1,0:T(4,128)(2,1)S(1)} %reshape.344, f32[10,4,64]{2,1,0:T(4,128)S(1)} %fusion.2, f32[10,4,64]{2,1,0:T(4,128)S(1)} %get-tuple-element.67, ...), kind=kOutput, calls=%fused_computation.8 | convolution fusion | flops 344719360 | bytes 19036240 | tf_op jit(solution)/shard_map/jhqd,jhskd->jhqsk/dot_general | solution.py:124
  265.1 1.5 multiply_bitcast_fusion
  267.4 6.2 %maximum_bitcast_fusion = f32[2,10,8,64,4,128]{5,3,2,4,1,0:T(8,128)S(1)} fusion(f32[1,10,4,8,64,128]{5,4,3,2,1,0:T(8,128)} %convolution_bitcast_fusion, f32[1,10,4,8,64,128]{5,4,3,2,1,0:T(8,128)S(1)} %multiply_bitcast_fusion), kind=kLoop, calls=%fused_computation.3 | loop fusion | flops 5242880 | bytes 41943040 | tf_op jit(solution)/shard_map/transpose | solution.py:140
  273.7 7.1 %copy-done = f32[2,10,8,64,4,128]{5,3,2,4,1,0:T(8,128)} copy-done((f32[2,10,8,64,4,128]{5,3,2,4,1,0:T(8,128)}, f32[2,10,8,64,4,128]{5,3,2,4,1,0:T(8,128)S(1)}, u32[]{:S(2)}) %copy-start) | copy-done | bytes 20971544
  282.3 7.6 %fusion.26 = f32[640,4096]{1,0:T(8,128)} fusion(bf16[512,4096]{1,0:T(8,128)(2,1)} %bitcast.201, bf16[80,8,4,128]{3,2,1,0:T(4,128)(2,1)S(1)} %bitcast.205), kind=kOutput, calls=%fused_computation.55 | convolution fusion | flops 2684354560 | bytes 15335424 | tf_op jit(solution)/shard_map/dot_general | solution.py:110
  289.9 4.3 slice.220
  295.1 2.7 copy.164
  297.8 4.2 broadcast_in_dim.37
  302.1 11.3 %scatter_fusion = bf16[2,48,64,4,128]{4,2,3,1,0:T(8,128)(2,1)} fusion(bf16[2,48,64,4,128]{4,2,3,1,0:T(8,128)(2,1)} %broadcast_in_dim.37, s32[30]{0:T(128)S(1)} %get-tuple-element.65, bf16[30,2,64,4,128]{4,2,3,1,0:T(8,128)(2,1)} %copy.164), kind=kCustom, calls=%fused_computation.2 | custom fusion | bytes 11796600 | tf_op jit(solution)/shard_map/scatter | solution.py:167
  313.3 8.3 %copy.165 = bf16[2,16,3,64,4,128]{5,3,4,2,0,1:T(8,128)(2,1)} copy(bf16[2,16,3,64,4,128]{5,3,4,2,1,0:T(8,128)(2,1)} %bitcast.191) | data formatting | bytes 12582912 | tf_op jit(solution)/shard_map/reshape | solution.py:170
  321.6 5.2 %all-to-all-start = ((bf16[2,16,3,64,4,128]{5,3,4,2,0,1:T(8,128)(2,1)}), bf16[2,16,3,64,4,128]{5,3,4,2,0,1:T(8,128)(2,1)}, u32[]{:S(2)}, u32[]{:S(2)}) async-start(bf16[2,16,3,64,4,128]{5,3,4,2,0,1:T(8,128)(2,1)} %copy.165), calls=%async_computation.1 | async-start | bytes 12582912 | tf_op jit(solution)/shard_map/all_to_all | solution.py:169
  328.0 4.3 slice_bitcast_fusion.10
  333.4 3.4 collective-permute-start.2
  336.8 1.3 collective-permute-start.3
  338.2 4.4 fusion.25
  342.6 1.3 copy.174
  344.6 36.4 %collective-permute-done.2 = bf16[2,64,4,128]{3,1,2,0:T(8,128)(2,1)S(1)} collective-permute-done((bf16[2,64,4,128]{3,1,2,0:T(8,128)(2,1)S(1)}, bf16[2,64,4,128]{3,1,2,0:T(8,128)(2,1)S(1)}, u32[]{:S(2)}, u32[]{:S(2)}) %collective-permute-start.2) | collective-permute-done | bytes 131104 | tf_op jit(solution)/shard_map/ppermute | solution.py:20
  381.0 3.8 collective-permute-done.3
  384.9 34.4 %all-reduce.4.cloned.1.call-done = bf16[2,2,64,4,128]{4,1,3,2,0:T(2,128)(2,1)} async-done(((bf16[2,2,64,4,128]{4,1,3,2,0:T(2,128)(2,1)}), bf16[2,2,64,4,128]{4,1,3,2,0:T(2,128)(2,1)}) %all-reduce.4.cloned.1.call-update) | async-done | bytes 262160 | tf_op jit(solution)/shard_map/psum | solution.py:153
  419.3 3.8 fusion.54
  423.1 7.9 %all-to-all-done = bf16[2,16,3,64,4,128]{5,3,4,2,0,1:T(8,128)(2,1)} async-done(((bf16[2,16,3,64,4,128]{5,3,4,2,0,1:T(8,128)(2,1)}), bf16[2,16,3,64,4,128]{5,3,4,2,0,1:T(8,128)(2,1)}, u32[]{:S(2)}, u32[]{:S(2)}) %all-to-all-start) | async-done | bytes 6291488 | tf_op jit(solution)/shard_map/all_to_all | solution.py:169
  431.0 4.3 copy.166
  435.3 6.2 %fusion.3 = f32[2,64,4,128,10]{3,4,2,1,0:T(8,128)S(1)} fusion(bf16[2,48,64,4,128]{4,2,3,1,0:T(8,128)(2,1)S(1)} %bitcast.194, s32[48]{0:T(128)S(1)} %eq.87, pred[48]{0:T(512)(128)(4,1)S(1)} %and.88), kind=kOutput, calls=%fused_computation.13 | convolution fusion | flops 62915520 | bytes 8913136 | tf_op jit(solution)/shard_map/mb,xmkhd->xbkhd/dot_general | solution.py:180
  441.5 3.3 fusion.10
  445.0 1.3 copy.176
  446.4 1.3 copy.175
  447.7 39.6 %reduce-scatter.2.cloned.1.call-done = f32[640,512]{1,0:T(8,128)} async-done(((f32[640,4096]{1,0:T(8,128)}), f32[640,512]{1,0:T(8,128)}) %reduce-scatter.2.cloned.1.call-update) | async-done | bytes 1310736 | tf_op jit(solution)/shard_map/reduce_scatter | solution.py:111
  487.3 2.2 convert_element_type.64
  (79 shorter events, 11.5 us)
Async XLA Ops:
  7.2 9.0 %copy-start.7 = (s32[160]{0:T(256)S(1)}, s32[160]{0:T(256)}, u32[]{:S(2)}) copy-start(s32[160]{0:T(256)} %param.19) | copy-start | bytes 1924
  7.2 9.0 %copy-start.5 = (s32[160,3]{0,1:T(4,128)S(1)}, s32[160,3]{0,1:T(4,128)}, u32[]{:S(2)}) copy-start(s32[160,3]{0,1:T(4,128)} %param.18) | copy-start | bytes 5764
  7.2 9.9 %copy-start.6 = (s32[2]{0:T(128)S(1)}, s32[2]{0:T(128)}, u32[]{:S(2)}) copy-start(s32[2]{0:T(128)} %param.17) | copy-start | bytes 28
  7.2 42.9 %all-gather.5.cloned.1.call-start = ((), (), s32[]{:S(2)}) async-start(), calls=%async_computation.4 | async-start | bytes 5898240 | tf_op jit(solution)/shard_map/all_gather | solution.py:115
  7.9 176.4 %all-gather.3.cloned.1.call-start = ((), (), s32[]{:S(2)}) async-start(), calls=%async_computation.2 | async-start | bytes 22282240 | tf_op jit(solution)/shard_map/all_gather | solution.py:71
  10.7 408.6 %all-reduce.4.cloned.1.call-start = ((), (), s32[]{:S(2)}) async-start(), calls=%async_computation.5 | async-start | bytes 524288 | tf_op jit(solution)/shard_map/psum | solution.py:153
  10.8 6.6 %collective-permute-start = (bf16[2,64,4,128]{3,1,2,0:T(8,128)(2,1)S(1)}, bf16[2,64,4,128]{3,1,2,0:T(8,128)(2,1)S(1)}, u32[]{:S(2)}, u32[]{:S(2)}) collective-permute-start(bf16[2,64,4,128]{3,1,2,0:T(8,128)(2,1)S(1)} %get-tuple-element.62), channel_id=1, source_target_pairs={{0,8},{8,16},{16,24},{24,32},{32,40},{40,48},{48,56},{56,64},{64,7... | collective-permute-start | bytes 393224 | tf_op jit(solution)/shard_map/ppermute | solution.py:20
  14.8 5.7 %collective-permute-start.1 = (bf16[2,64,4,128]{3,1,2,0:T(8,128)(2,1)S(1)}, bf16[2,64,4,128]{3,1,2,0:T(8,128)(2,1)S(1)}, u32[]{:S(2)}, u32[]{:S(2)}) collective-permute-start(bf16[2,64,4,128]{3,1,2,0:T(8,128)(2,1)S(1)} %get-tuple-element.63), channel_id=1, source_target_pairs={{8,0},{16,8},{24,16},{32,24},{40,32},{48,40},{56,48},{64,56},{72,6... | collective-permute-start | bytes 393224 | tf_op jit(solution)/shard_map/ppermute | solution.py:21
  219.3 7.5 %copy-start.4 = (bf16[640,4,128]{2,1,0:T(4,128)(2,1)S(1)}, bf16[640,4,128]{2,1,0:T(4,128)(2,1)}, u32[]{:S(2)}) copy-start(bf16[640,4,128]{2,1,0:T(4,128)(2,1)} %param.12) | copy-start | bytes 1966084
  231.0 3.9 copy-start.3
  265.1 2.4 copy-start.2
  273.7 7.1 %copy-start = (f32[2,10,8,64,4,128]{5,3,2,4,1,0:T(8,128)}, f32[2,10,8,64,4,128]{5,3,2,4,1,0:T(8,128)S(1)}, u32[]{:S(2)}) copy-start(f32[2,10,8,64,4,128]{5,3,2,4,1,0:T(8,128)S(1)} %maximum_bitcast_fusion) | copy-start | bytes 62914564
  282.2 205.1 %reduce-scatter.2.cloned.1.call-start = ((), (), s32[]{:S(2)}) async-start(), calls=%async_computation.3 | async-start | bytes 11796480 | tf_op jit(solution)/shard_map/reduce_scatter | solution.py:111
  321.6 16.5 %slice-start = ((s8[5242880]{0:T(1024)(128)(4,1)}), s8[1048576]{0:T(1024)(128)(4,1)S(1)}, s32[]{:S(2)}) async-start(s8[5242880]{0:T(1024)(128)(4,1)} %bitcast.198), calls=%async_computation.6 | async-start | bytes 2097152
  321.6 109.4 %all-to-all-start = ((bf16[2,16,3,64,4,128]{5,3,4,2,0,1:T(8,128)(2,1)}), bf16[2,16,3,64,4,128]{5,3,4,2,0,1:T(8,128)(2,1)}, u32[]{:S(2)}, u32[]{:S(2)}) async-start(bf16[2,16,3,64,4,128]{5,3,4,2,0,1:T(8,128)(2,1)} %copy.165), calls=%async_computation.1 | async-start | bytes 12582912 | tf_op jit(solution)/shard_map/all_to_all | solution.py:169
  328.0 10.2 %slice-start.1 = ((s8[5242880]{0:T(1024)(128)(4,1)}), s8[4194304]{0:T(1024)(128)(4,1)S(1)}, s32[]{:S(2)}) async-start(s8[5242880]{0:T(1024)(128)(4,1)} %bitcast.198), calls=%async_computation.7 | async-start | bytes 8388608
  333.4 47.6 %collective-permute-start.2 = (bf16[2,64,4,128]{3,1,2,0:T(8,128)(2,1)S(1)}, bf16[2,64,4,128]{3,1,2,0:T(8,128)(2,1)S(1)}, u32[]{:S(2)}, u32[]{:S(2)}) collective-permute-start(bf16[2,64,4,128]{3,1,2,0:T(8,128)(2,1)S(1)} %get-tuple-element.55), channel_id=1, source_target_pairs={{0,8},{8,16},{16,24},{24,32},{32,40},{40,48},{48,56},{56,64},{64,7... | collective-permute-start | bytes 393224 | tf_op jit(solution)/shard_map/ppermute | solution.py:20
  336.8 47.9 %collective-permute-start.3 = (bf16[2,64,4,128]{3,1,2,0:T(8,128)(2,1)S(1)}, bf16[2,64,4,128]{3,1,2,0:T(8,128)(2,1)S(1)}, u32[]{:S(2)}, u32[]{:S(2)}) collective-permute-start(bf16[2,64,4,128]{3,1,2,0:T(8,128)(2,1)S(1)} %get-tuple-element.56), channel_id=1, source_target_pairs={{8,0},{16,8},{24,16},{32,24},{40,32},{48,40},{56,48},{64,56},{72,6... | collective-permute-start | bytes 393224 | tf_op jit(solution)/shard_map/ppermute | solution.py:21
  435.3 6.3 %copy-start.1 = (f32[2,64,4,128,10]{3,4,2,1,0:T(8,128)S(1)}, f32[2,64,4,128,10]{3,4,2,1,0:T(8,128)}, u32[]{:S(2)}) copy-start(f32[2,64,4,128,10]{3,4,2,1,0:T(8,128)} %fusion.54) | copy-start | bytes 7864324
Sparse Core Ops, SparseCore 0:
  9.7 40.3 all-gather.4
  52.2 132.0 all-gather.2
  282.4 136.8 all-reduce.3
  421.7 65.5 reduce-scatter.1
where the time goes:
time: 504 us; the launch traced here: 496 us
  waiting for transfers between devices  277 us (55%)
  local copies, waits for them, and re-layouts  109 us (22%)
  matrix products  60.9 us (12%)
  other arithmetic  18.5 us (4%)
  starting transfers between devices  15.4 us (3%)
  between operations  14.7 us (3%)
    all_gather x1, waiting for transfers between devices, local(): everything = lax.all_gather(stacked, 'ctx', axis=1, tiled=True)  127 us
    reduce_scatter x1, waiting for transfers between devices, local(): lax.psum_scatter(partial_out, 'head', scatter_dimension=1, tiled=True)  39.6 us
    ppermute x2, waiting for transfers between devices, with_halo(): before = lax.ppermute(last, axis, up)  36.4 us
    psum x1, waiting for transfers between devices, local(): lax.psum(global_sums.astype(jnp.bfloat16), 'ctx').astype(jnp.float32)  34.4 us
    all_gather x1, waiting for transfers between devices, local(): lax.all_gather(out_grad, 'head', axis=1, tiled=True)  24.1 us
    unnamed x29, local copies, waits for them, and re-layouts  22.9 us
    reshape x1, local copies, waits for them, and re-layouts, local(): all_blocks = everything.reshape((2, blocks_all) + tail_shape)  17.5 us
    scatter x1, local copies, waits for them, and re-layouts, local(): back_buffer = jnp.zeros((2, shards * capacity) + tail_shape, jnp.bfloat16...  11.3 us
  transfers between devices with their start and end apart: 9, of which 8 were waited for; matrix products, arithmetic and copies ran while one was open for 18% of the time, Pallas kernels for 0%

commit v1 on v0

v1 whole, which is shorter than its diff:
```python
import functools
import math

import jax
import jax.numpy as jnp
from jax import lax
from jax.experimental import pallas as pl
from jax.experimental.pallas import tpu as pltpu
from jax.sharding import PartitionSpec as P

SIDE = 4
BLOCK = 64
G = 2
R = 3
HERE = 640
NBD = 10
HD = 128
HPD = 4
NB = 160
SHARD = 512
MESH = pl.DeviceIdType.MESH
NT = (((1,), (1,)), ((), ()))
TN = (((0,), (0,)), ((), ()))
DZ = (1, 3, 2)


def place():
    ctx, hd = lax.axis_index("ctx"), lax.axis_index("head")
    return ctx, hd, ctx // SIDE, lax.rem(ctx, SIDE), hd // 2, lax.rem(hd, 2)


def query_row(y, c):
    return y * (1 - c) + (3 - y) * c


def remote(src, dst, send, recv, device):
    return pltpu.make_async_remote_copy(
        src_ref=src, dst_ref=dst, send_sem=send, recv_sem=recv, device_id=device, device_id_type=MESH
    )


def greet(device):
    pl.semaphore_signal(pltpu.get_barrier_semaphore(), inc=1, device_id=device, device_id_type=MESH)


def rows_of(index):
    return pl.ds(pl.multiple_of(index * HERE, HERE), HERE)


def gather_kernel(
    kvq, og, w, ka, va, qa, doa,
    ogv, acc, dov,
    ks, kr, fs, fr, qs, qr, ds, dr, zs, zr, cs, cr, own,
):
    ctx, hd, x, y, z, c = place()
    half = y // 2
    other = {"head": 2 * z + 1 - c}
    cw = lax.rem(half + c, 2)
    yw = query_row(y, cw)
    src_half = lax.rem(half + c, 2)
    other_half = lax.rem(half + 1 - c, 2)
    ys = query_row(y, c)
    to_self = 1 - jnp.minimum(c + half, 1)

    def worker(k, b):
        return {"ctx": k * SIDE + 2 * c + b, "head": 2 * z + cw}

    def query_worker(k):
        return {"ctx": k * SIDE + yw, "head": 2 * z + cw}

    def source(xs, t):
        return {"ctx": xs * SIDE + 2 * src_half + t, "head": 2 * z + half}

    for dx in range(SIDE):
        xs = lax.rem(x + dx, SIDE)
        for t in range(2):
            if dx:
                greet(source(xs, t))
            else:
                mine = (2 * src_half + t == y) & (half == c)

                @pl.when(jnp.logical_not(mine))
                def _():
                    greet(source(xs, t))
    for dz in DZ:
        greet({"head": 2 * lax.rem(z + dz, SIDE) + c})
    greet(other)
    pl.semaphore_wait(pltpu.get_barrier_semaphore(), 12 - to_self)

    local = pltpu.make_async_copy(og, ogv.at[hd], own)
    local.start()
    core = [remote(og, ogv.at[hd], cs.at[0], cr.at[0], other)]
    core[0].start()
    sends = []
    for i, dz in ((2, 2), (0, 1), (1, 3)):
        for q in range(4):
            part = pl.ds(q * 160, 160)
            copy = remote(
                og.at[part], ogv.at[hd, part], zs.at[i, q], zr.at[i, q],
                {"head": 2 * lax.rem(z + dz, SIDE) + c},
            )
            copy.start()
            sends.append(copy)

    slot = x * 2 + lax.rem(y, 2)
    own_sends = []
    for dx in (2, 1, 3, 0):
        k = lax.rem(x + dx, SIDE)
        for t, dst in ((0, ka), (1, va)):
            for b in range(2):
                copy = remote(
                    kvq.at[k, t], dst.at[rows_of(ctx)], ks.at[dx, b, t], kr.at[slot, t], worker(k, b)
                )
                if dx:
                    copy.start()
                    sends.append(copy)
                else:
                    mine = (2 * c + b == y) & (cw == c)
                    here = pltpu.make_async_copy(kvq.at[k, t], dst.at[rows_of(ctx)], kr.at[slot, t])
                    pl.when(jnp.logical_not(mine))(copy.start)
                    pl.when(mine)(here.start)
                    own_sends.append((copy, mine))
    for dx in (2, 1, 3, 0):
        k = lax.rem(x + dx, SIDE)
        copy = remote(kvq.at[k, 2], qa.at[rows_of(x)], qs.at[dx], qr.at[x], query_worker(k))
        if dx:
            copy.start()
            sends.append(copy)
        else:
            mine = (yw == y) & (cw == c)
            here = pltpu.make_async_copy(kvq.at[k, 2], qa.at[rows_of(x)], qr.at[x])
            pl.when(jnp.logical_not(mine))(copy.start)
            pl.when(mine)(here.start)
            own_sends.append((copy, mine))

    acc[...] = jnp.zeros_like(acc)

    def add_shard(s):
        columns = pl.ds(pl.multiple_of(s * SHARD, SHARD), SHARD)

        def tile(i, carry):
            part = pl.ds(pl.multiple_of(i * 128, 128), 128)
            acc[part, :] += lax.dot_general(
                ogv[s, part, :], w[:, columns], NT, preferred_element_type=jnp.float32
            )
            return carry

        lax.fori_loop(0, HERE // 128, tile, 0)

    def forward(j):
        xs, t2 = j // 2, j % 2
        idx = xs * SIDE + 2 * src_half + t2
        for t, dst in ((0, ka), (1, va)):
            part = dst.at[rows_of(idx)]
            remote(part, part, fs.at[j, t], kr.at[j, t], other).wait_recv()
            copy = remote(part, part, fs.at[j, t], fr.at[j, t], other)
            copy.start()
            sends.append(copy)

    local.wait()
    add_shard(hd)
    core[0].wait_recv()
    add_shard(2 * z + 1 - c)
    for i in range(3):
        zp = lax.rem(z + SIDE - DZ[i], SIDE)
        s = 2 * zp + c
        for q in range(4):
            part = pl.ds(q * 160, 160)
            view = ogv.at[s, part]
            remote(view, view, zs.at[i, q], zr.at[i, q], other).wait_recv()
        copy = remote(ogv.at[s], ogv.at[s], cs.at[1 + i], cr.at[1 + i], other)
        copy.start()
        core.append(copy)
        add_shard(s)
    for i in range(3):
        zp = lax.rem(z + SIDE - DZ[i], SIDE)
        core[1 + i].wait_recv()
        add_shard(2 * zp + 1 - c)
    for k in range(HPD):
        dov[k] = acc[:, k * HD : (k + 1) * HD].astype(jnp.bfloat16)
    for dx in (2, 1, 3, 0):
        k = lax.rem(x + dx, SIDE)
        copy = remote(dov.at[k], doa.at[rows_of(x)], ds.at[dx], dr.at[x], query_worker(k))
        if dx:
            copy.start()
            sends.append(copy)
        else:
            mine = (yw == y) & (cw == c)
            here = pltpu.make_async_copy(dov.at[k], doa.at[rows_of(x)], dr.at[x])
            pl.when(jnp.logical_not(mine))(copy.start)
            pl.when(mine)(here.start)
            own_sends.append((copy, mine))
    for j in range(8):
        forward(j)
    for xs in range(SIDE):
        part = qa.at[rows_of(xs)]
        remote(part, part, qs.at[0], qr.at[xs], other).wait_recv()
        part = doa.at[rows_of(xs)]
        remote(part, part, ds.at[0], dr.at[xs], other).wait_recv()
    for j in range(8):
        idx = (j // 2) * SIDE + 2 * other_half + j % 2
        for t, dst in ((0, ka), (1, va)):
            part = dst.at[rows_of(idx)]
            remote(part, part, fs.at[j, t], fr.at[j, t], other).wait_recv()
    for copy in sends + core:
        copy.wait_send()
    for copy, mine in own_sends:
        pl.when(jnp.logical_not(mine))(copy.wait_send)


def attention_kernel(rid, rcnt, gid, q, do, k, v, o, dq, dk, dv, dka, dva, dkg, dvg):
    ctx, hd, x, y, z, c = place()
    ys = query_row(y, c)
    scale = 1.0 / math.sqrt(HD)
    f32 = jnp.float32
    dka[...] = jnp.zeros_like(dka)
    dva[...] = jnp.zeros_like(dva)
    dkg[...] = jnp.zeros_like(dkg)
    dvg[...] = jnp.zeros_like(dvg)

    def span(block, count):
        return pl.ds(pl.multiple_of(block * BLOCK, BLOCK), count * BLOCK)

    g0, g1 = span(gid[0], 1), span(gid[1], 1)
    column = lax.broadcasted_iota(jnp.int32, (1, 8 * BLOCK), 1) // BLOCK

    def step(n, carry):
        xs = n // NBD
        i = (xs * SIDE + ys) * NBD + (n - xs * NBD)
        first = jnp.clip(i - 1, 0, NB - 3)
        window = span(first, 3)
        randoms = [span(rid[i * R + r], 1) for r in range(R)]
        count = rcnt[i]
        kc = jnp.concatenate([k[window, :], k[g0, :], k[g1, :]] + [k[r, :] for r in randoms], axis=0)
        vc = jnp.concatenate([v[window, :], v[g0, :], v[g1, :]] + [v[r, :] for r in randoms], axis=0)
        mine = span(n, 1)
        qn, dn = q[mine, :], do[mine, :]
        low, high = i - 1 - first, i + 1 - first
        keep = ((column >= low) & (column <= high)) | ((column >= 3) & (column < 5 + count))
        keep = keep & ((column <= high) | (column >= 3))
        s = lax.dot_general(qn, kc, NT, preferred_element_type=f32) * scale
        s = jnp.where(keep, s, -1e30)
        peak = jnp.max(s, axis=1, keepdims=True)
        e = jnp.exp(s - peak)
        p = e / jnp.sum(e, axis=1, keepdims=True)
        low_p = p.astype(jnp.bfloat16)
        on = jnp.dot(low_p, vc, preferred_element_type=f32).astype(jnp.bfloat16)
        o[mine, :] = on
        delta = jnp.sum(dn.astype(f32) * on.astype(f32), axis=1, keepdims=True)
        dp = lax.dot_general(dn, vc, NT, preferred_element_type=f32)
        dsc = (p * (dp - delta)).astype(jnp.bfloat16)
        dq[mine, :] = (jnp.dot(dsc, kc, preferred_element_type=f32) * scale).astype(jnp.bfloat16)
        dkt = lax.dot_general(dsc, qn, TN, preferred_element_type=f32)
        dvt = lax.dot_general(low_p, dn, TN, preferred_element_type=f32)
        for total, glob, term in ((dka, dkg, dkt), (dva, dvg, dvt)):
            total[window, :] += term[: 3 * BLOCK]
            glob[...] += term[3 * BLOCK : 5 * BLOCK]
            for r in range(R):
                total[randoms[r], :] += term[(5 + r) * BLOCK : (6 + r) * BLOCK]
        return carry

    lax.fori_loop(0, 4 * NBD, step, 0)
    for total, glob in ((dka, dkg), (dva, dvg)):
        total[g0, :] += glob[:BLOCK]
        total[g1, :] += glob[BLOCK:]

    def finish(n, carry):
        part = pl.ds(pl.multiple_of(n * 256, 256), 256)
        dk[part, :] = (dka[part, :] * scale).astype(jnp.bfloat16)
        dv[part, :] = dva[part, :].astype(jnp.bfloat16)
        return carry

    lax.fori_loop(0, NB * BLOCK // 256, finish, 0)


def return_kernel(
    oa, dqa, dka, dva, w, proj, dqh, dkh, dvh,
    oh, part_out, core_in, z_in, last, dmine, dcore, dhome,
    os, orr, qs, qr, es, er, ls, hs, hr, cs, cr, zs, zr,
):
    ctx, hd, x, y, z, c = place()
    f32 = jnp.float32
    half = y // 2
    other = {"head": 2 * z + 1 - c}
    cw = lax.rem(half + c, 2)
    src_half = lax.rem(half + c, 2)
    other_half = lax.rem(half + 1 - c, 2)
    ys = query_row(y, c)
    to_self = 1 - jnp.minimum(c + half, 1)

    def home(xs, yy):
        return {"ctx": xs * SIDE + yy, "head": 2 * z + half}

    def worker(k, b):
        return {"ctx": k * SIDE + 2 * c + b, "head": 2 * z + cw}

    for dx in range(SIDE):
        k = lax.rem(x + dx, SIDE)
        for b in range(2):
            if dx:
                greet(worker(k, b))
            else:
                mine = (2 * c + b == y) & (cw == c)

                @pl.when(jnp.logical_not(mine))
                def _():
                    greet(worker(k, b))
    for dz in DZ:
        greet({"head": 2 * lax.rem(z + dz, SIDE) + c})
    greet(other)
    pl.semaphore_wait(pltpu.get_barrier_semaphore(), 12 - to_self)

    sends, own_sends = [], []

    def send_home(src, dst, send, recv, dx, yy):
        copy = remote(src, dst, send, recv, home(lax.rem(x + dx, SIDE), yy))
        if dx:
            copy.start()
            sends.append(copy)
        else:
            mine = (yy == y) & (half == c)
            here = pltpu.make_async_copy(src, dst, recv)
            pl.when(jnp.logical_not(mine))(copy.start)
            pl.when(mine)(here.start)
            own_sends.append((copy, mine))

    for dx in (2, 1, 3, 0):
        xs = lax.rem(x + dx, SIDE)
        send_home(oa.at[rows_of(xs)], oh.at[x], os.at[dx], orr.at[x], dx, ys)
    loads = []
    for j in range(8):
        idx = (j // 2) * SIDE + 2 * other_half + j % 2
        mid = (j // 2) * SIDE + 2 * src_half + j % 2
        for t, src in ((0, dka), (1, dva)):
            copy = remote(src.at[rows_of(idx)], dcore.at[j, t], es.at[j, t], er.at[j, t], other)
            copy.start()
            sends.append(copy)
            copy = pltpu.make_async_copy(src.at[rows_of(mid)], dmine.at[j, t], ls.at[j, t])
            copy.start()
            loads.append(copy)
    for dx in (2, 1, 3, 0):
        xs = lax.rem(x + dx, SIDE)
        send_home(dqa.at[rows_of(xs)], dqh.at[x], qs.at[dx], qr.at[x], dx, ys)

    b = lax.rem(y, 2)
    for dx in (2, 1, 3, 0):
        xs = lax.rem(x + dx, SIDE)
        for t2 in range(2):
            j = xs * 2 + t2
            for t in range(2):
                pltpu.make_async_copy(dmine.at[j, t], dmine.at[j, t], ls.at[j, t]).wait()
                remote(dcore.at[j, t], dcore.at[j, t], es.at[j, t], er.at[j, t], other).wait_recv()
                dmine[j, t] = (dmine[j, t].astype(f32) + dcore[j, t].astype(f32)).astype(jnp.bfloat16)
                send_home(
                    dmine.at[j, t], dhome.at[x, b, t], hs.at[dx, t2, t], hr.at[x, b, t],
                    dx, 2 * src_half + t2,
                )

    for k in range(HPD):
        remote(oh.at[k], oh.at[k], os.at[0], orr.at[k], other).wait_recv()

    def shard_product(s, put):
        columns = pl.ds(pl.multiple_of(s * SHARD, SHARD), SHARD)

        def tile(i, carry):
            part = pl.ds(pl.multiple_of(i * 128, 128), 128)
            rows = jnp.concatenate([oh[k, part, :] for k in range(HPD)], axis=1)
            put(part, jnp.dot(rows, w[:, columns], preferred_element_type=f32))
            return carry

        lax.fori_loop(0, HERE // 128, tile, 0)

    for i, dz in enumerate((2, 1, 3, 0)):
        zp = lax.rem(z + dz, SIDE)

        def put(part, value):
            part_out[i, part, :] = value.astype(jnp.bfloat16)

        shard_product(2 * zp + 1 - c, put)
        copy = remote(part_out.at[i], core_in.at[i], cs.at[i], cr.at[i], other)
        copy.start()
        sends.append(copy)
    for i, dz in enumerate((2, 1, 3)):
        zp = lax.rem(z + dz, SIDE)
        remote(core_in.at[i], core_in.at[i], cs.at[i], cr.at[i], other).wait_recv()

        def put(part, value):
            part_out[4 + i, part, :] = (value + core_in[i, part, :].astype(f32)).astype(jnp.bfloat16)

        shard_product(2 * zp + c, put)
        copy = remote(part_out.at[4 + i], z_in.at[i], zs.at[i], zr.at[i], {"head": 2 * zp + c})
        copy.start()
        sends.append(copy)
    remote(core_in.at[3], core_in.at[3], cs.at[3], cr.at[3], other).wait_recv()

    def put(part, value):
        last[part, :] = value + core_in[3, part, :].astype(f32)

    shard_product(hd, put)

    for k in range(HPD):
        for t, out in ((0, dkh), (1, dvh)):
            for bb in range(2):
                view = dhome.at[k, bb, t]
                remote(view, view, hs.at[0, 0, 0], hr.at[k, bb, t], other).wait_recv()
            out[k] = (dhome[k, 0, t].astype(f32) + dhome[k, 1, t].astype(f32)).astype(jnp.bfloat16)
    for i in range(3):
        remote(z_in.at[i], z_in.at[i], zs.at[i], zr.at[i], other).wait_recv()
        if i < 2:
            last[...] += z_in[i].astype(f32)
        else:
            proj[...] = (last[...] + z_in[i].astype(f32)).astype(jnp.bfloat16)
    for k in range(HPD):
        remote(dqh.at[k], dqh.at[k], qs.at[0], qr.at[k], other).wait_recv()
    for copy in sends:
        copy.wait_send()
    for copy, mine in own_sends:
        pl.when(jnp.logical_not(mine))(copy.wait_send)


ANY = pl.BlockSpec(memory_space=pl.ANY)
VMEM = pl.BlockSpec(memory_space=pltpu.VMEM)
SMEM = pl.BlockSpec(memory_space=pltpu.SMEM)
LIMIT = 56 * 1024 * 1024


def struct(*shape):
    return jax.ShapeDtypeStruct(shape, jnp.bfloat16)


def sem(*shape):
    return pltpu.SemaphoreType.DMA(shape)


def local(queries, key_rows, value_rows, out_weight, out_grad, global_ids, random_ids, random_count):
    bf16, f32 = jnp.bfloat16, jnp.float32
    kvq = jnp.transpose(jnp.stack([key_rows, value_rows, queries], axis=0), (2, 0, 1, 3))
    w = out_weight.reshape(HPD * HD, out_weight.shape[2])
    tokens = NB * BLOCK
    ka, va, qa, doa = pl.pallas_call(
        gather_kernel,
        out_shape=(struct(tokens, HD), struct(tokens, HD), struct(4 * HERE, HD), struct(4 * HERE, HD)),
        in_specs=[ANY, ANY, VMEM],
        out_specs=(ANY,) * 4,
        scratch_shapes=[
            pltpu.VMEM((8, HERE, SHARD), bf16),
            pltpu.VMEM((HERE, SHARD), f32),
            pltpu.VMEM((HPD, HERE, HD), bf16),
            sem(4, 2, 2), sem(8, 2), sem(8, 2), sem(8, 2), sem(4), sem(4), sem(4), sem(4),
            sem(3, 4), sem(3, 4), sem(4), sem(4), pltpu.SemaphoreType.DMA,
        ],
        compiler_params=pltpu.CompilerParams(
            collective_id=0, has_side_effects=True, vmem_limit_bytes=LIMIT
        ),
    )(kvq, out_grad, w)
    oa, dqa, dka, dva = pl.pallas_call(
        attention_kernel,
        out_shape=(struct(4 * HERE, HD), struct(4 * HERE, HD), struct(tokens, HD), struct(tokens, HD)),
        in_specs=[SMEM] * 3 + [VMEM] * 4,
        out_specs=(VMEM,) * 4,
        scratch_shapes=[
            pltpu.VMEM((tokens, HD), f32),
            pltpu.VMEM((tokens, HD), f32),
            pltpu.VMEM((2 * BLOCK, HD), f32),
            pltpu.VMEM((2 * BLOCK, HD), f32),
        ],
        compiler_params=pltpu.CompilerParams(vmem_limit_bytes=LIMIT),
    )(random_ids.reshape(NB * R), random_count, global_ids, qa, doa, ka, va)
    projected, dqh, dkh, dvh = pl.pallas_call(
        return_kernel,
        out_shape=(struct(HERE, SHARD),) + (struct(HPD, HERE, HD),) * 3,
        in_specs=[ANY] * 4 + [VMEM],
        out_specs=(VMEM, ANY, VMEM, VMEM),
        scratch_shapes=[
            pltpu.VMEM((HPD, HERE, HD), bf16),
            pltpu.VMEM((7, HERE, SHARD), bf16),
            pltpu.VMEM((4, HERE, SHARD), bf16),
            pltpu.VMEM((3, HERE, SHARD), bf16),
            pltpu.VMEM((HERE, SHARD), f32),
            pltpu.VMEM((8, 2, HERE, HD), bf16),
            pltpu.VMEM((8, 2, HERE, HD), bf16),
            pltpu.VMEM((HPD, 2, 2, HERE, HD), bf16),
            sem(4), sem(4), sem(4), sem(4), sem(8, 2), sem(8, 2), sem(8, 2),
            sem(4, 2, 2), sem(4, 2, 2), sem(4), sem(4), sem(3), sem(3),
        ],
        compiler_params=pltpu.CompilerParams(
            collective_id=1, has_side_effects=True, vmem_limit_bytes=LIMIT
        ),
    )(oa, dqa, dka, dva, w)
    grads = [jnp.transpose(g, (1, 0, 2)) for g in (dqh, dkh, dvh)]
    return (projected, *grads)


def solution(mesh):
    placed = (
        P("ctx", "head", None),
        P("ctx", "head", None),
        P("ctx", "head", None),
        P("head", None, None),
        P("ctx", "head"),
        P(),
        P(),
        P(),
    )
    return jax.shard_map(
        local,
        mesh=mesh,
        in_specs=placed,
        out_specs=(
            P("ctx", "head"),
            P("ctx", "head", None),
            P("ctx", "head", None),
            P("ctx", "head", None),
        ),
        check_vma=False,
    )
```

time: 504 us -> 180 us (0.36)
  the two profiles are of different devices: /device:TPU:1 before, /device:TPU:19 now
where the time goes in v1:
time: 180 us
  Pallas kernels  166 us (92%)
  local copies, waits for them, and re-layouts  11.4 us (6%)
    pallas_call x1, Pallas kernels, local(): pl.pallas_call(return_kernel, out_shape=(struct(HERE, SHARD),) + (struct(...  68.3 us
    pallas_call x1, Pallas kernels, local(): pl.pallas_call(gather_kernel, out_shape=(struct(tokens, HD), struct(token...  57.9 us
    pallas_call x1, Pallas kernels, local(): pl.pallas_call(attention_kernel, out_shape=(struct(4 * HERE, HD), struct(...  40.3 us
    unnamed x10, local copies, waits for them, and re-layouts  9.11 us

profile of v1, /device:TPU:19, one launch (start us, length us, event | category | flops | bytes accessed | tf_op | source)
XLA Modules:
  0.0 180.0 jit_solution(1667110597363630511)
XLA Ops:
  0.6 0.8 copy.18
  1.4 0.8 reshape.14.rid
  2.2 1.2 copy.28
  3.4 1.5 copy_bitcast_fusion
  4.9 1.5 maximum_bitcast_fusion.kvq
  6.4 57.9 %shard_map.111 = (bf16[10240,128]{1,0:T(8,128)(2,1)}, bf16[10240,128]{1,0:T(8,128)(2,1)}, bf16[2560,128]{1,0:T(8,128)(2,1)}, bf16[2560,128]{1,0:T(8,128)(2,1)}) custom-call(bf16[4,3,640,128]{3,2,1,0:T(8,128)(2,1)} %maximum_bitcast_fusion.kvq, bf16[640,512]{1,0:T(8,128)(2,1)} %og.1, bf16[512,4096]{1,0:T(8,128)(2,1)} %bitcast.13), custom_call_target="tpu_custom_call" | custom-call | tf_op jit(solution)/shard_map/pallas_call | solution.py:440
  64.3 40.3 %shard_map.112 = (bf16[2560,128]{1,0:T(8,128)(2,1)}, bf16[2560,128]{1,0:T(8,128)(2,1)}, bf16[10240,128]{1,0:T(8,128)(2,1)}, bf16[10240,128]{1,0:T(8,128)(2,1)}) custom-call(s32[480]{0:T(512)} %reshape.14.rid, s32[160]{0:T(256)} %rcnt.1, s32[2]{0:T(128)} %gid.1, bf16[2560,128]{1,0:T(8,128)(2,1)} %get-tuple-element.16.q, ...), custom_call_target="tpu_custom_call" | custom-call | tf_op jit(solution)/shard_map/pallas_call | solution.py:456
  104.6 68.3 %shard_map.113 = (bf16[640,512]{1,0:T(8,128)(2,1)}, bf16[4,640,128]{2,1,0:T(8,128)(2,1)}, bf16[4,640,128]{2,1,0:T(8,128)(2,1)}, bf16[4,640,128]{2,1,0:T(8,128)(2,1)}) custom-call(bf16[2560,128]{1,0:T(8,128)(2,1)} %get-tuple-element.20.oa, bf16[2560,128]{1,0:T(8,128)(2,1)} %get-tuple-element.21.dqa, bf16[10240,128]{1,0:T(8,128)(2,1)} %get-tuple-element.22.dka, ...), custom_call_target="tpu_custom_call" | custom-call | tf_op jit(solution)/shard_map/pallas_call | solution.py:469
  172.9 0.0 copy-start.1
  172.9 0.0 copy-start
  172.9 2.5 %copy.22 = bf16[640,4,128]{2,1,0:T(4,128)(2,1)} copy(bf16[640,4,128]{2,0,1:T(8,128)(2,1)} %bitcast.18) | data formatting | bytes 1310720
  175.4 2.4 %copy.23 = bf16[640,4,128]{2,1,0:T(4,128)(2,1)} copy(bf16[640,4,128]{2,0,1:T(8,128)(2,1)} %bitcast.17) | data formatting | bytes 1310720
  177.9 0.0 copy-done.1
  177.9 1.3 copy.24
  179.2 0.0 copy-done
  179.2 0.8 copy.30
Async XLA Ops:
  172.9 5.0 %copy-start.1 = (bf16[4,640,128]{2,1,0:T(8,128)(2,1)S(1)}, bf16[4,640,128]{2,1,0:T(8,128)(2,1)}, u32[]{:S(2)}) copy-start(bf16[4,640,128]{2,1,0:T(8,128)(2,1)} %get-tuple-element.27) | copy-start | bytes 1966084
  172.9 6.3 %copy-start = (bf16[640,512]{1,0:T(8,128)(2,1)S(1)}, bf16[640,512]{1,0:T(8,128)(2,1)}, u32[]{:S(2)}) copy-start(bf16[640,512]{1,0:T(8,128)(2,1)} %get-tuple-element.42) | copy-start | bytes 1966084

commit v2 on v1

v2 whole, which is shorter than its diff:
```python
import functools
import math

import jax
import jax.numpy as jnp
from jax import lax
from jax.experimental import pallas as pl
from jax.experimental.pallas import tpu as pltpu
from jax.sharding import PartitionSpec as P

SIDE = 4
BLOCK = 64
G = 2
R = 3
HERE = 640
NBD = 10
HD = 128
HPD = 4
NB = 160
SHARD = 512
MESH = pl.DeviceIdType.MESH
NT = (((1,), (1,)), ((), ()))
TN = (((0,), (0,)), ((), ()))


def place():
    ctx, hd = lax.axis_index("ctx"), lax.axis_index("head")
    return ctx, hd, ctx // SIDE, lax.rem(ctx, SIDE), hd // 2, lax.rem(hd, 2)


def query_row(y, c):
    return y * (1 - c) + (3 - y) * c


def remote(src, dst, send, recv, device):
    return pltpu.make_async_remote_copy(
        src_ref=src, dst_ref=dst, send_sem=send, recv_sem=recv, device_id=device, device_id_type=MESH
    )


def greet(device):
    pl.semaphore_signal(pltpu.get_barrier_semaphore(), inc=1, device_id=device, device_id_type=MESH)


def rows_of(index):
    return pl.ds(pl.multiple_of(index * HERE, HERE), HERE)


def neighbours(x, y, z, c):
    pair = {"ctx": x * SIDE + y + 1 - 2 * lax.rem(y, 2)}
    other = {"head": 2 * z + 1 - c}
    up = {"head": 2 * lax.rem(z + 1, SIDE) + c}
    down = {"head": 2 * lax.rem(z + 3, SIDE) + c}
    return pair, other, up, down


def enter(senders, to_self):
    for device, mine in senders:
        if mine is None:
            greet(device)
        else:
            pl.when(jnp.logical_not(mine))(functools.partial(greet, device))
    pl.semaphore_wait(pltpu.get_barrier_semaphore(), len(senders) - to_self)


class Sends:
    def __init__(self):
        self.started, self.guarded = [], []

    def start(self, copy):
        copy.start()
        self.started.append(copy)

    def start_unless(self, mine, src, dst, send, recv, device):
        copy = remote(src, dst, send, recv, device)
        here = pltpu.make_async_copy(src, dst, recv)
        pl.when(jnp.logical_not(mine))(copy.start)
        pl.when(mine)(here.start)
        self.guarded.append((copy, mine))

    def wait(self):
        for copy in self.started:
            copy.wait_send()
        for copy, mine in self.guarded:
            pl.when(jnp.logical_not(mine))(copy.wait_send)


QUARTER = HERE // 4


def quarter(q):
    return pl.ds(q * QUARTER, QUARTER)


def gather_kernel(
    kvq, og, w, ka, va, qa, doa,
    ogv, acc, dov,
    ks, kr, ps, pr, fs, fr, ds, dr, zs, zr, cs, cr, own,
):
    ctx, hd, x, y, z, c = place()
    half = y // 2
    pair, other, up, down = neighbours(x, y, z, c)
    cw = lax.rem(half + c, 2)
    yw = query_row(y, cw)
    py = y + 1 - 2 * lax.rem(y, 2)
    near, pair_near = query_row(y, c), query_row(py, c)
    other_near, other_pair_near = query_row(y, 1 - c), query_row(py, 1 - c)
    to_self = 1 - jnp.minimum(c + half, 1)
    me = to_self == 1

    def worker(k):
        return {"ctx": k * SIDE + yw, "head": 2 * z + cw}

    senders = [
        ({"ctx": lax.rem(x + dx, SIDE) * SIDE + near, "head": 2 * z + half}, None if dx else me)
        for dx in range(SIDE)
    ]
    enter(senders + [(up, None), (down, None), (other, None), (pair, None)], to_self)

    sends = Sends()

    def send_worker(src, dst, send, recv, dx, k):
        if dx:
            sends.start(remote(src, dst, send, recv, worker(k)))
        else:
            sends.start_unless(me, src, dst, send, recv, worker(k))

    def arrived(view, recv):
        remote(view, view, recv, recv, other).wait_recv()

    local = pltpu.make_async_copy(og, ogv.at[hd], own)
    local.start()
    for dx in (0, 1, 3, 2):
        k = lax.rem(x + dx, SIDE)
        for t, dst in ((0, ka), (1, va)):
            send_worker(kvq.at[k, t], dst.at[rows_of(ctx)], ks.at[dx, t], kr.at[x, t], dx, k)
        if dx == 0:
            for q in range(4):
                for i, to, p in ((0, up, q), (1, down, (q + 2) % 4)):
                    sends.start(
                        remote(og.at[quarter(p)], ogv.at[hd, quarter(p)], zs.at[i, p], zr.at[i, p], to)
                    )
            sends.start(remote(og, ogv.at[hd], cs.at[0], cr.at[0], other))
    for dx in (0, 1, 3, 2):
        k = lax.rem(x + dx, SIDE)
        send_worker(kvq.at[k, 2], qa.at[rows_of(x)], ks.at[dx, 2], kr.at[x, 2], dx, k)

    def add_shard(s):
        columns = pl.ds(pl.multiple_of(s * SHARD, SHARD), SHARD)

        def tile(i, carry):
            part = pl.ds(pl.multiple_of(i * 128, 128), 128)
            acc[part, :] += lax.dot_general(
                ogv[s, part, :], w[:, columns], NT, preferred_element_type=jnp.float32
            )
            return carry

        lax.fori_loop(0, HERE // 128, tile, 0)

    def pass_near(dx):
        xs = lax.rem(x + SIDE - dx, SIDE)
        for t, dst in ((0, ka), (1, va)):
            view = dst.at[rows_of(xs * SIDE + near)]
            arrived(view, kr.at[xs, t])
            sends.start(remote(view, view, ps.at[xs, t], pr.at[xs, t], pair))
            sends.start(remote(view, view, fs.at[xs, t], fr.at[xs, t], other))

    def pass_pair(dx):
        xs = lax.rem(x + SIDE - dx, SIDE)
        for t, dst in ((0, ka), (1, va)):
            view = dst.at[rows_of(xs * SIDE + pair_near)]
            arrived(view, pr.at[xs, t])
            sends.start(remote(view, view, fs.at[4 + xs, t], fr.at[4 + xs, t], other))

    below = 2 * lax.rem(z + 3, SIDE)
    above = 2 * lax.rem(z + 1, SIDE)
    across = 2 * lax.rem(z + 2, SIDE)

    pass_near(0)
    for q in range(2):
        for i, s, to, p in ((0, below, up, q), (1, above, down, q + 2)):
            view = ogv.at[s + c, quarter(p)]
            arrived(view, zr.at[i, p])
            sends.start(remote(view, view, zs.at[2, p], zr.at[2, p], to))
    pass_near(1)
    pass_near(3)
    acc[...] = jnp.zeros_like(acc)
    local.wait()
    add_shard(hd)
    arrived(ogv.at[2 * z + 1 - c], cr.at[0])
    add_shard(2 * z + 1 - c)
    pass_near(2)
    pass_pair(0)
    for i, s in ((0, below), (1, above)):
        for q in range(2):
            p = q + 2 - 2 * i
            arrived(ogv.at[s + c, quarter(p)], zr.at[i, p])
        sends.start(remote(ogv.at[s + c], ogv.at[s + c], cs.at[1 + i], cr.at[1 + i], other))
        add_shard(s + c)
    for i, s in ((0, below), (1, above)):
        arrived(ogv.at[s + 1 - c], cr.at[1 + i])
        add_shard(s + 1 - c)
    pass_pair(1)
    for p in range(4):
        arrived(ogv.at[across + c, quarter(p)], zr.at[2, p])
    sends.start(remote(ogv.at[across + c], ogv.at[across + c], cs.at[3], cr.at[3], other))
    add_shard(across + c)
    arrived(ogv.at[across + 1 - c], cr.at[3])
    add_shard(across + 1 - c)
    for k in range(HPD):
        dov[k] = acc[:, k * HD : (k + 1) * HD].astype(jnp.bfloat16)
    for dx in (2, 1, 3, 0):
        k = lax.rem(x + dx, SIDE)
        send_worker(dov.at[k], doa.at[rows_of(x)], ds.at[dx], dr.at[x], dx, k)
    pass_pair(3)
    pass_pair(2)
    for xs in range(SIDE):
        arrived(qa.at[rows_of(xs)], kr.at[xs, 2])
        arrived(doa.at[rows_of(xs)], dr.at[xs])
        for t, dst in ((0, ka), (1, va)):
            arrived(dst.at[rows_of(xs * SIDE + other_near)], fr.at[xs, t])
            arrived(dst.at[rows_of(xs * SIDE + other_pair_near)], fr.at[4 + xs, t])
    sends.wait()


UNROLL = 5


def attention_kernel(rid, rcnt, gid, q, do, k, v, o, dq, dk, dv, dka, dva, dkg, dvg):
    ctx, hd, x, y, z, c = place()
    ys = query_row(y, c)
    scale = 1.0 / math.sqrt(HD)
    f32, bf16 = jnp.float32, jnp.bfloat16
    dka[...] = jnp.zeros_like(dka)
    dva[...] = jnp.zeros_like(dva)
    dkg[...] = jnp.zeros_like(dkg)
    dvg[...] = jnp.zeros_like(dvg)

    def span(block, count):
        return pl.ds(pl.multiple_of(block * BLOCK, BLOCK), count * BLOCK)

    g0, g1 = span(gid[0], 1), span(gid[1], 1)
    column = lax.broadcasted_iota(jnp.int32, (1, 8 * BLOCK), 1) // BLOCK

    def listed(ref, window, randoms):
        return jnp.concatenate([ref[window, :], ref[g0, :], ref[g1, :]] + [ref[r, :] for r in randoms], axis=0)

    def step(m, carry):
        work = []
        for u in range(UNROLL):
            n = m * UNROLL + u
            xs = n // NBD
            i = (xs * SIDE + ys) * NBD + (n - xs * NBD)
            first = jnp.clip(i - 1, 0, NB - 3)
            window = span(first, 3)
            randoms = [span(rid[i * R + r], 1) for r in range(R)]
            low, high = i - 1 - first, i + 1 - first
            keep = ((column >= low) & (column <= high) & (column < 3)) | (
                (column >= 3) & (column < 5 + rcnt[i])
            )
            bias = jnp.where(keep, 0.0, -1e30).astype(f32)
            work.append((span(n, 1), window, randoms, bias))
        kc = [listed(k, window, randoms) for _, window, randoms, _ in work]
        vc = [listed(v, window, randoms) for _, window, randoms, _ in work]
        qn = [q[mine, :] for mine, _, _, _ in work]
        dn = [do[mine, :] for mine, _, _, _ in work]
        s = [
            lax.dot_general(a, b, NT, preferred_element_type=f32) * scale + t[3]
            for a, b, t in zip(qn, kc, work)
        ]
        dp = [lax.dot_general(a, b, NT, preferred_element_type=f32) for a, b in zip(dn, vc)]
        e = [jnp.exp(a - jnp.max(a, axis=1, keepdims=True)) for a in s]
        p = [a * (1.0 / jnp.sum(a, axis=1, keepdims=True)) for a in e]
        low_p = [a.astype(bf16) for a in p]
        on = [jnp.dot(a, b, preferred_element_type=f32).astype(bf16) for a, b in zip(low_p, vc)]
        delta = [
            jnp.sum(a.astype(f32) * b.astype(f32), axis=1, keepdims=True) for a, b in zip(dn, on)
        ]
        dsc = [(a * (b - d)).astype(bf16) for a, b, d in zip(p, dp, delta)]
        dvt = [lax.dot_general(a, b, TN, preferred_element_type=f32) for a, b in zip(low_p, dn)]
        dkt = [lax.dot_general(a, b, TN, preferred_element_type=f32) for a, b in zip(dsc, qn)]
        dqn = [
            (jnp.dot(a, b, preferred_element_type=f32) * scale).astype(bf16) for a, b in zip(dsc, kc)
        ]
        for t, a, b in zip(work, on, dqn):
            o[t[0], :] = a
            dq[t[0], :] = b
        for total, glob, terms in ((dka, dkg, dkt), (dva, dvg, dvt)):
            glob[...] += sum(a[3 * BLOCK : 5 * BLOCK] for a in terms)
            for (_, window, randoms, _), a in zip(work, terms):
                total[window, :] += a[: 3 * BLOCK]
                for r in range(R):
                    total[randoms[r], :] += a[(5 + r) * BLOCK : (6 + r) * BLOCK]
        return carry

    lax.fori_loop(0, 4 * NBD // UNROLL, step, 0)
    for total, glob in ((dka, dkg), (dva, dvg)):
        total[g0, :] += glob[:BLOCK]
        total[g1, :] += glob[BLOCK:]

    def finish(n, carry):
        part = pl.ds(pl.multiple_of(n * 256, 256), 256)
        dk[part, :] = (dka[part, :] * scale).astype(bf16)
        dv[part, :] = dva[part, :].astype(bf16)
        return carry

    lax.fori_loop(0, NB * BLOCK // 256, finish, 0)


def return_kernel(
    oa, dqa, dka, dva, w, proj, dqh, dkh, dvh,
    oh, part_out, core_in, hop_in, z_in, held, dmine, dcore, dpair,
    os, orr, qs, qr, es, er, ls, ps, pr, hs, hr, cs, cr, as_, ar, zs, zr,
):
    ctx, hd, x, y, z, c = place()
    f32, bf16 = jnp.float32, jnp.bfloat16
    half = y // 2
    pair, other, up, down = neighbours(x, y, z, c)
    cw = lax.rem(half + c, 2)
    yw = query_row(y, cw)
    py = y + 1 - 2 * lax.rem(y, 2)
    near, pair_near = query_row(y, c), query_row(py, c)
    other_near, other_pair_near = query_row(y, 1 - c), query_row(py, 1 - c)
    to_self = 1 - jnp.minimum(c + half, 1)
    me = to_self == 1

    senders = [
        ({"ctx": lax.rem(x + dx, SIDE) * SIDE + yw, "head": 2 * z + cw}, None if dx else me)
        for dx in range(SIDE)
    ]
    enter(senders + [(up, None), (down, None), (other, None), (pair, None)], to_self)

    sends = Sends()

    def send_home(src, dst, send, recv, dx):
        home = {"ctx": lax.rem(x + dx, SIDE) * SIDE + near, "head": 2 * z + half}
        if dx:
            sends.start(remote(src, dst, send, recv, home))
        else:
            sends.start_unless(me, src, dst, send, recv, home)

    def arrived(view, recv):
        remote(view, view, recv, recv, other).wait_recv()

    for dx in (2, 1, 3, 0):
        send_home(oa.at[rows_of(lax.rem(x + dx, SIDE))], oh.at[x], os.at[dx], orr.at[x], dx)
    for g, there, here in ((0, other_pair_near, pair_near), (4, other_near, near)):
        for dx in (2, 1, 3, 0):
            xs = lax.rem(x + dx, SIDE)
            for t, src in ((0, dka), (1, dva)):
                j = g + xs
                sends.start(
                    remote(src.at[rows_of(xs * SIDE + there)], dcore.at[j, t], es.at[j, t], er.at[j, t], other)
                )
                pltpu.make_async_copy(
                    src.at[rows_of(xs * SIDE + here)], dmine.at[j, t], ls.at[j, t]
                ).start()
    for dx in (2, 1, 3, 0):
        send_home(dqa.at[rows_of(lax.rem(x + dx, SIDE))], dqh.at[x], qs.at[dx], qr.at[x], dx)

    def cores_met(j, t):
        pltpu.make_async_copy(dmine.at[j, t], dmine.at[j, t], ls.at[j, t]).wait()
        arrived(dcore.at[j, t], er.at[j, t])

    for dx in (2, 1, 3, 0):
        xs = lax.rem(x + dx, SIDE)
        for t in range(2):
            cores_met(xs, t)
            dmine[xs, t] = (dmine[xs, t].astype(f32) + dcore[xs, t].astype(f32)).astype(bf16)
            sends.start(remote(dmine.at[xs, t], dpair.at[xs, t], ps.at[xs, t], pr.at[xs, t], pair))

    def finish(dx):
        xs = lax.rem(x + dx, SIDE)
        for t, out in ((0, dkh), (1, dvh)):
            cores_met(4 + xs, t)
            arrived(dpair.at[xs, t], pr.at[xs, t])
            dmine[4 + xs, t] = (
                dmine[4 + xs, t].astype(f32) + dcore[4 + xs, t].astype(f32) + dpair[xs, t].astype(f32)
            ).astype(bf16)
            send_home(dmine.at[4 + xs, t], out.at[x], hs.at[dx, t], hr.at[x, t], dx)

    for k in range(HPD):
        arrived(oh.at[k], orr.at[k])

    def shard_product(s, put):
        columns = pl.ds(pl.multiple_of(s * SHARD, SHARD), SHARD)

        def tile(i, carry):
            part = pl.ds(pl.multiple_of(i * QUARTER, QUARTER), QUARTER)
            rows = jnp.concatenate([oh[k, part, :] for k in range(HPD)], axis=1)
            put(part, jnp.dot(rows, w[:, columns], preferred_element_type=f32))
            return carry

        lax.fori_loop(0, 4, tile, 0)

    below = 2 * lax.rem(z + 3, SIDE)
    above = 2 * lax.rem(z + 1, SIDE)
    across = 2 * lax.rem(z + 2, SIDE)

    for i, s in enumerate((across, above, below, 2 * z)):

        def put(part, value):
            part_out[i, part, :] = value.astype(bf16)

        shard_product(s + 1 - c, put)
        sends.start(remote(part_out.at[i], core_in.at[i], cs.at[i], cr.at[i], other))

    arrived(core_in.at[0], cr.at[0])

    def put_across(part, value):
        part_out[4, part, :] = (value + core_in[0, part, :].astype(f32)).astype(bf16)

    shard_product(across + c, put_across)
    for q in range(4):
        sends.start(
            remote(
                part_out.at[4, quarter(q)], hop_in.at[quarter(q)], as_.at[q], ar.at[q], up if q < 2 else down
            )
        )
    for i, s, to in ((0, above, up), (1, below, down)):
        arrived(core_in.at[1 + i], cr.at[1 + i])

        def put_near(part, value):
            part_out[5 + i, part, :] = (value + core_in[1 + i, part, :].astype(f32)).astype(bf16)

        shard_product(s + c, put_near)
        for q in (2 - 2 * i, 3 - 2 * i):
            sends.start(
                remote(part_out.at[5 + i, quarter(q)], z_in.at[i, quarter(q)], zs.at[i, q], zr.at[i, q], to)
            )
    arrived(core_in.at[3], cr.at[3])

    def put_own(part, value):
        held[part, :] = value + core_in[3, part, :].astype(f32)

    shard_product(hd, put_own)
    finish(2)
    for q in range(2):
        for i, to in ((0, up), (1, down)):
            p = q + 2 * i
            arrived(hop_in.at[quarter(p)], ar.at[p])
            part_out[5 + i, quarter(p), :] = (
                part_out[5 + i, quarter(p), :].astype(f32) + hop_in[quarter(p), :].astype(f32)
            ).astype(bf16)
            sends.start(
                remote(part_out.at[5 + i, quarter(p)], z_in.at[i, quarter(p)], zs.at[i, p], zr.at[i, p], to)
            )
    for dx in (1, 3, 0):
        finish(dx)
    for i in range(2):
        for q in range(4):
            arrived(z_in.at[i, quarter(q)], zr.at[i, q])
    proj[...] = (held[...] + z_in[0].astype(f32) + z_in[1].astype(f32)).astype(bf16)
    for k in range(HPD):
        arrived(dqh.at[k], qr.at[k])
        arrived(dkh.at[k], hr.at[k, 0])
        arrived(dvh.at[k], hr.at[k, 1])
    sends.wait()


ANY = pl.BlockSpec(memory_space=pl.ANY)
VMEM = pl.BlockSpec(memory_space=pltpu.VMEM)
SMEM = pl.BlockSpec(memory_space=pltpu.SMEM)
LIMIT = 56 * 1024 * 1024


def struct(*shape):
    return jax.ShapeDtypeStruct(shape, jnp.bfloat16)


def sem(*shape):
    return pltpu.SemaphoreType.DMA(shape)


def local(queries, key_rows, value_rows, out_weight, out_grad, global_ids, random_ids, random_count):
    bf16, f32 = jnp.bfloat16, jnp.float32
    kvq = jnp.transpose(jnp.stack([key_rows, value_rows, queries], axis=0), (2, 0, 1, 3))
    w = out_weight.reshape(HPD * HD, out_weight.shape[2])
    tokens = NB * BLOCK
    ka, va, qa, doa = pl.pallas_call(
        gather_kernel,
        out_shape=(struct(tokens, HD), struct(tokens, HD), struct(4 * HERE, HD), struct(4 * HERE, HD)),
        in_specs=[ANY, ANY, VMEM],
        out_specs=(ANY,) * 4,
        scratch_shapes=[
            pltpu.VMEM((8, HERE, SHARD), bf16),
            pltpu.VMEM((HERE, SHARD), f32),
            pltpu.VMEM((HPD, HERE, HD), bf16),
            sem(4, 3), sem(4, 3), sem(4, 2), sem(4, 2), sem(8, 2), sem(8, 2), sem(4), sem(4),
            sem(3, 4), sem(3, 4), sem(4), sem(4), pltpu.SemaphoreType.DMA,
        ],
        compiler_params=pltpu.CompilerParams(
            collective_id=0, has_side_effects=True, vmem_limit_bytes=LIMIT
        ),
    )(kvq, out_grad, w)
    oa, dqa, dka, dva = pl.pallas_call(
        attention_kernel,
        out_shape=(struct(4 * HERE, HD), struct(4 * HERE, HD), struct(tokens, HD), struct(tokens, HD)),
        in_specs=[SMEM] * 3 + [VMEM] * 4,
        out_specs=(VMEM,) * 4,
        scratch_shapes=[
            pltpu.VMEM((tokens, HD), f32),
            pltpu.VMEM((tokens, HD), f32),
            pltpu.VMEM((2 * BLOCK, HD), f32),
            pltpu.VMEM((2 * BLOCK, HD), f32),
        ],
        compiler_params=pltpu.CompilerParams(vmem_limit_bytes=LIMIT),
    )(random_ids.reshape(NB * R), random_count, global_ids, qa, doa, ka, va)
    projected, dqh, dkh, dvh = pl.pallas_call(
        return_kernel,
        out_shape=(struct(HERE, SHARD),) + (struct(HPD, HERE, HD),) * 3,
        in_specs=[ANY] * 4 + [VMEM],
        out_specs=(VMEM, ANY, ANY, ANY),
        scratch_shapes=[
            pltpu.VMEM((HPD, HERE, HD), bf16),
            pltpu.VMEM((7, HERE, SHARD), bf16),
            pltpu.VMEM((4, HERE, SHARD), bf16),
            pltpu.VMEM((HERE, SHARD), bf16),
            pltpu.VMEM((2, HERE, SHARD), bf16),
            pltpu.VMEM((HERE, SHARD), f32),
            pltpu.VMEM((8, 2, HERE, HD), bf16),
            pltpu.VMEM((8, 2, HERE, HD), bf16),
            pltpu.VMEM((4, 2, HERE, HD), bf16),
            sem(4), sem(4), sem(4), sem(4), sem(8, 2), sem(8, 2), sem(8, 2), sem(4, 2), sem(4, 2),
            sem(4, 2), sem(4, 2), sem(4), sem(4), sem(4), sem(4), sem(2, 4), sem(2, 4),
        ],
        compiler_params=pltpu.CompilerParams(
            collective_id=1, has_side_effects=True, vmem_limit_bytes=LIMIT
        ),
    )(oa, dqa, dka, dva, w)
    grads = [jnp.transpose(g, (1, 0, 2)) for g in (dqh, dkh, dvh)]
    return (projected, *grads)


def solution(mesh):
    placed = (
        P("ctx", "head", None),
        P("ctx", "head", None),
        P("ctx", "head", None),
        P("head", None, None),
        P("ctx", "head"),
        P(),
        P(),
        P(),
    )
    return jax.shard_map(
        local,
        mesh=mesh,
        in_specs=placed,
        out_specs=(
            P("ctx", "head"),
            P("ctx", "head", None),
            P("ctx", "head", None),
            P("ctx", "head", None),
        ),
        check_vma=False,
    )
```

time: 180 us -> 134 us (0.74)
  the two profiles are of different devices: /device:TPU:19 before, /device:TPU:1 now
where the time goes in v2:
time: 134 us
  Pallas kernels  120 us (90%)
  local copies, waits for them, and re-layouts  11.4 us (9%)
  other arithmetic  1.52 us (1%)
    pallas_call x1, Pallas kernels, local(): pl.pallas_call(gather_kernel, out_shape=(struct(tokens, HD), struct(token...  56.3 us
    pallas_call x1, Pallas kernels, local(): pl.pallas_call(return_kernel, out_shape=(struct(HERE, SHARD),) + (struct(...  43.8 us
    pallas_call x1, Pallas kernels, local(): pl.pallas_call(attention_kernel, out_shape=(struct(4 * HERE, HD), struct(...  20.2 us
    unnamed x10, local copies, waits for them, and re-layouts  9.11 us

profile of v2, /device:TPU:1, one launch (start us, length us, event | category | flops | bytes accessed | tf_op | source)
XLA Modules:
  0.0 133.9 jit_solution(16083122693340386161)
XLA Ops:
  0.6 0.8 copy.18
  1.4 0.8 reshape.14.rid
  2.2 1.2 copy.28
  3.4 1.5 %copy_bitcast_fusion = (bf16[1,640,4,128]{3,1,0,2:T(8,128)(2,1)S(1)}, bf16[1,640,4,128]{3,1,0,2:T(8,128)(2,1)S(1)}) fusion(bf16[640,4,128]{2,1,0:T(4,128)(2,1)} %param.8, bf16[640,4,128]{2,1,0:T(4,128)(2,1)} %param.10), kind=kLoop, calls=%fused_computation.1 | loop fusion | bytes 2621440 | tf_op jit(solution)/shard_map/stack | solution.py:477
  4.9 1.5 %maximum_bitcast_fusion.kvq = bf16[4,3,640,128]{3,2,1,0:T(8,128)(2,1)} fusion(bf16[1,640,4,128]{3,1,0,2:T(8,128)(2,1)S(1)} %get-tuple-element.36, bf16[1,640,4,128]{3,1,0,2:T(8,128)(2,1)S(1)} %get-tuple-element.37, bf16[1,640,4,128]{3,1,0,2:T(8,128)(2,1)S(1)} %bitcast.15), kind=kLoop, calls=%fused_computation | loop fusion | flops 1966080 | bytes 3932160 | tf_op jit(solution)/shard_map/transpose | solution.py:477
  6.4 56.3 %shard_map.111 = (bf16[10240,128]{1,0:T(8,128)(2,1)}, bf16[10240,128]{1,0:T(8,128)(2,1)}, bf16[2560,128]{1,0:T(8,128)(2,1)}, bf16[2560,128]{1,0:T(8,128)(2,1)}) custom-call(bf16[4,3,640,128]{3,2,1,0:T(8,128)(2,1)} %maximum_bitcast_fusion.kvq, bf16[640,512]{1,0:T(8,128)(2,1)} %og.1, bf16[512,4096]{1,0:T(8,128)(2,1)} %bitcast.13), custom_call_target="tpu_custom_call" | custom-call | tf_op jit(solution)/shard_map/pallas_call | solution.py:480
  62.7 20.2 %shard_map.112 = (bf16[2560,128]{1,0:T(8,128)(2,1)}, bf16[2560,128]{1,0:T(8,128)(2,1)}, bf16[10240,128]{1,0:T(8,128)(2,1)}, bf16[10240,128]{1,0:T(8,128)(2,1)}) custom-call(s32[480]{0:T(512)} %reshape.14.rid, s32[160]{0:T(256)} %rcnt.1, s32[2]{0:T(128)} %gid.1, bf16[2560,128]{1,0:T(8,128)(2,1)} %get-tuple-element.16.q, ...), custom_call_target="tpu_custom_call" | custom-call | tf_op jit(solution)/shard_map/pallas_call | solution.py:496
  82.9 43.8 %shard_map.113 = (bf16[640,512]{1,0:T(8,128)(2,1)}, bf16[4,640,128]{2,1,0:T(8,128)(2,1)}, bf16[4,640,128]{2,1,0:T(8,128)(2,1)}, bf16[4,640,128]{2,1,0:T(8,128)(2,1)}) custom-call(bf16[2560,128]{1,0:T(8,128)(2,1)} %get-tuple-element.20.oa, bf16[2560,128]{1,0:T(8,128)(2,1)} %get-tuple-element.21.dqa, bf16[10240,128]{1,0:T(8,128)(2,1)} %get-tuple-element.22.dka, ...), custom_call_target="tpu_custom_call" | custom-call | tf_op jit(solution)/shard_map/pallas_call | solution.py:509
  126.7 0.0 copy-start.1
  126.8 0.0 copy-start
  126.8 2.5 %copy.22 = bf16[640,4,128]{2,1,0:T(4,128)(2,1)} copy(bf16[640,4,128]{2,0,1:T(8,128)(2,1)} %bitcast.18) | data formatting | bytes 1310720
  129.3 2.4 %copy.23 = bf16[640,4,128]{2,1,0:T(4,128)(2,1)} copy(bf16[640,4,128]{2,0,1:T(8,128)(2,1)} %bitcast.17) | data formatting | bytes 1310720
  131.7 0.0 copy-done.1
  131.7 1.3 %copy.24 = bf16[640,4,128]{2,1,0:T(4,128)(2,1)} copy(bf16[640,4,128]{2,0,1:T(8,128)(2,1)S(1)} %bitcast.16) | data formatting | bytes 1310720
  133.1 0.0 copy-done
  133.1 0.8 copy.30
Async XLA Ops:
  126.7 5.0 %copy-start.1 = (bf16[4,640,128]{2,1,0:T(8,128)(2,1)S(1)}, bf16[4,640,128]{2,1,0:T(8,128)(2,1)}, u32[]{:S(2)}) copy-start(bf16[4,640,128]{2,1,0:T(8,128)(2,1)} %get-tuple-element.27) | copy-start | bytes 1966084
  126.8 6.3 %copy-start = (bf16[640,512]{1,0:T(8,128)(2,1)S(1)}, bf16[640,512]{1,0:T(8,128)(2,1)}, u32[]{:S(2)}) copy-start(bf16[640,512]{1,0:T(8,128)(2,1)} %get-tuple-element.42) | copy-start | bytes 1966084

commit v3 on v2

v3 whole, which is shorter than its diff:
```python
import functools
import math

import jax
import jax.numpy as jnp
from jax import lax
from jax.experimental import pallas as pl
from jax.experimental.pallas import tpu as pltpu
from jax.sharding import PartitionSpec as P

SIDE = 4
BLOCK = 64
G = 2
R = 3
HERE = 640
NBD = 10
HD = 128
HPD = 4
NB = 160
SHARD = 512
MESH = pl.DeviceIdType.MESH
NT = (((1,), (1,)), ((), ()))
TN = (((0,), (0,)), ((), ()))


def place():
    ctx, hd = lax.axis_index("ctx"), lax.axis_index("head")
    return ctx, hd, ctx // SIDE, lax.rem(ctx, SIDE), hd // 2, lax.rem(hd, 2)


def query_row(y, c):
    return y * (1 - c) + (3 - y) * c


def remote(src, dst, send, recv, device):
    return pltpu.make_async_remote_copy(
        src_ref=src, dst_ref=dst, send_sem=send, recv_sem=recv, device_id=device, device_id_type=MESH
    )


def greet(device):
    pl.semaphore_signal(pltpu.get_barrier_semaphore(), inc=1, device_id=device, device_id_type=MESH)


def blocks_of(index):
    return pl.ds(index * NBD, NBD)


PIECES = 2
PIECE = HERE // PIECES
CUT = NBD // PIECES


def padded(index, h):
    return pl.ds(1 + index * NBD + h * CUT, CUT)


def pieces(*refs):
    return [(t * PIECES + h, h, t, ref) for h in range(PIECES) for t, ref in enumerate(refs)]


def neighbours(x, y, z, c):
    pair = {"ctx": x * SIDE + y + 1 - 2 * lax.rem(y, 2)}
    other = {"head": 2 * z + 1 - c}
    up = {"head": 2 * lax.rem(z + 1, SIDE) + c}
    down = {"head": 2 * lax.rem(z + 3, SIDE) + c}
    return pair, other, up, down


def enter(senders, to_self):
    for device, mine in senders:
        if mine is None:
            greet(device)
        else:
            pl.when(jnp.logical_not(mine))(functools.partial(greet, device))
    pl.semaphore_wait(pltpu.get_barrier_semaphore(), len(senders) - to_self)


class Sends:
    def __init__(self):
        self.started, self.guarded = [], []

    def start(self, copy):
        copy.start()
        self.started.append(copy)

    def start_unless(self, mine, src, dst, send, recv, device):
        copy = remote(src, dst, send, recv, device)
        here = pltpu.make_async_copy(src, dst, recv)
        pl.when(jnp.logical_not(mine))(copy.start)
        pl.when(mine)(here.start)
        self.guarded.append((copy, mine))

    def wait(self):
        for copy in self.started:
            copy.wait_send()
        for copy, mine in self.guarded:
            pl.when(jnp.logical_not(mine))(copy.wait_send)


QUARTER = HERE // 4


def quarter(q):
    return pl.ds(q * QUARTER, QUARTER)


UNROLL = 5
MASKED = -1e30
NR = 4 * NBD * R
LAST = NR + G
LISTED = LAST + NB


def layer_kernel(
    aux, off, kvq, og, w, proj, dqh, dkh, dvh,
    ka, va, qa, doa, oa, dqa, ogv, acc, dov, wv, dka, dva, dkg, dvg, runk, runv,
    oh, core_in, hop_in, z_in, stage, dcore, psend, nsend, dpair,
    ks, kr, qs, qr, ps, pr, fs, fr, ds, dr, zs, zr, cs, cr, own, wsem,
    os, orr, gs, gr, es, er, bs, br, hs, hr, c2s, c2r, as_, ar, z2s, z2r,
):
    ctx, hd, x, y, z, c = place()
    f32, bf16 = jnp.float32, jnp.bfloat16
    half = y // 2
    pair, other, up, down = neighbours(x, y, z, c)
    cw = lax.rem(half + c, 2)
    yw = query_row(y, cw)
    py = y + 1 - 2 * lax.rem(y, 2)
    near, pair_near = query_row(y, c), query_row(py, c)
    other_near, other_pair_near = query_row(y, 1 - c), query_row(py, 1 - c)
    to_self = 1 - jnp.minimum(c + half, 1)
    me = to_self == 1

    def worker(k):
        return {"ctx": k * SIDE + yw, "head": 2 * z + cw}

    senders = [
        ({"ctx": lax.rem(x + dx, SIDE) * SIDE + near, "head": 2 * z + half}, None if dx else me)
        for dx in range(SIDE)
    ]
    local = pltpu.make_async_copy(og, ogv.at[hd], own)
    local.start()
    weight = pltpu.make_async_copy(w, wv, wsem)
    weight.start()
    receivers = [
        ({"ctx": lax.rem(x + dx, SIDE) * SIDE + yw, "head": 2 * z + cw}, None if dx else me)
        for dx in range(SIDE)
    ]
    enter(senders + receivers + [(up, None), (down, None), (other, None), (pair, None)], 2 * to_self)

    sends, early = Sends(), Sends()

    def send_worker(src, dst, send, recv, dx, k):
        if dx:
            sends.start(remote(src, dst, send, recv, worker(k)))
        else:
            sends.start_unless(me, src, dst, send, recv, worker(k))

    def arrived(view, recv):
        remote(view, view, recv, recv, other).wait_recv()

    def send_pieces(dxs):
        for m, h, t, dst in pieces(ka, va):
            for dx in dxs:
                k = lax.rem(x + dx, SIDE)
                src = kvq.at[k, t, pl.ds(h * CUT, CUT)]
                send_worker(src, dst.at[padded(ctx, h)], ks.at[dx, m], kr.at[x, m], dx, k)

    send_pieces((0,))
    for q in range(4):
        for i, to, p in ((0, up, q), (1, down, (q + 2) % 4)):
            sends.start(remote(og.at[quarter(p)], ogv.at[hd, quarter(p)], zs.at[i, p], zr.at[i, p], to))
    send_pieces((1, 3))
    sends.start(remote(og, ogv.at[hd], cs.at[0], cr.at[0], other))
    dka[...] = jnp.zeros_like(dka)
    dva[...] = jnp.zeros_like(dva)
    for ref in (dkg, dvg):
        ref[...] = jnp.zeros_like(ref)
    for ref in (ka, va):
        ref[0] = jnp.zeros((BLOCK, HD), bf16)
        ref[NB + 1] = jnp.zeros((BLOCK, HD), bf16)
    for ref in (runk, runv):
        ref[0] = jnp.zeros((BLOCK, HD), f32)

    def add_shard(s):
        columns = pl.ds(pl.multiple_of(s * SHARD, SHARD), SHARD)

        def tile(i, carry):
            part = pl.ds(pl.multiple_of(i * PIECE, PIECE), PIECE)
            acc[part, :] += lax.dot_general(
                ogv[s, part, :], wv[:, columns], NT, preferred_element_type=f32
            )
            return carry

        lax.fori_loop(0, PIECES, tile, 0)

    def pass_near(dxs):
        for m, h, t, dst in pieces(ka, va):
            for dx in dxs:
                xs = lax.rem(x + SIDE - dx, SIDE)
                view = dst.at[padded(xs * SIDE + near, h)]
                arrived(view, kr.at[xs, m])
                sends.start(remote(view, view, ps.at[xs, m], pr.at[xs, m], pair))
                sends.start(remote(view, view, fs.at[xs, m], fr.at[xs, m], other))

    def pass_pair(dx):
        xs = lax.rem(x + SIDE - dx, SIDE)
        for m, h, t, dst in pieces(ka, va):
            view = dst.at[padded(xs * SIDE + pair_near, h)]
            arrived(view, pr.at[xs, m])
            sends.start(remote(view, view, fs.at[4 + xs, m], fr.at[4 + xs, m], other))

    below = 2 * lax.rem(z + 3, SIDE)
    above = 2 * lax.rem(z + 1, SIDE)
    across = 2 * lax.rem(z + 2, SIDE)

    pass_near((0,))
    for q in range(2):
        for i, s, to, p in ((0, below, up, q), (1, above, down, q + 2)):
            view = ogv.at[s + c, quarter(p)]
            arrived(view, zr.at[i, p])
            early.start(remote(view, view, zs.at[2, p], zr.at[2, p], to))
    pass_near((1, 3))
    send_pieces((2,))
    for dx in (0, 1, 3, 2):
        k = lax.rem(x + dx, SIDE)
        send_worker(kvq.at[k, 2], qa.at[blocks_of(x)], qs.at[dx], qr.at[x], dx, k)
    acc[...] = jnp.zeros_like(acc)
    local.wait()
    weight.wait()
    add_shard(hd)
    arrived(ogv.at[2 * z + 1 - c], cr.at[0])
    add_shard(2 * z + 1 - c)
    pass_near((2,))
    pass_pair(0)
    for i, s in ((0, below), (1, above)):
        for q in range(2):
            p = q + 2 - 2 * i
            arrived(ogv.at[s + c, quarter(p)], zr.at[i, p])
        early.start(remote(ogv.at[s + c], ogv.at[s + c], cs.at[1 + i], cr.at[1 + i], other))
        add_shard(s + c)
    for i, s in ((0, below), (1, above)):
        arrived(ogv.at[s + 1 - c], cr.at[1 + i])
        add_shard(s + 1 - c)
    pass_pair(1)
    for p in range(4):
        arrived(ogv.at[across + c, quarter(p)], zr.at[2, p])
    early.start(remote(ogv.at[across + c], ogv.at[across + c], cs.at[3], cr.at[3], other))
    add_shard(across + c)
    arrived(ogv.at[across + 1 - c], cr.at[3])
    add_shard(across + 1 - c)
    for k in range(HPD):
        dov[k] = acc[:, k * HD : (k + 1) * HD].astype(bf16).reshape(NBD, BLOCK, HD)
    for dx in (2, 1, 3, 0):
        k = lax.rem(x + dx, SIDE)
        send_worker(dov.at[k], doa.at[blocks_of(x)], ds.at[dx], dr.at[x], dx, k)
    pass_pair(3)
    pass_pair(2)
    for xs in range(SIDE):
        arrived(qa.at[blocks_of(xs)], qr.at[xs])
        arrived(doa.at[blocks_of(xs)], dr.at[xs])
        for m, h, t, dst in pieces(ka, va):
            arrived(dst.at[padded(xs * SIDE + other_near, h)], fr.at[xs, m])
            arrived(dst.at[padded(xs * SIDE + other_pair_near, h)], fr.at[4 + xs, m])

    scale = 1.0 / math.sqrt(HD)

    def named(entry):
        return aux[LISTED + entry]

    g0, g1 = named(NR), named(NR + 1)
    column = lax.broadcasted_iota(jnp.int32, (1, 8 * BLOCK), 1) // BLOCK
    entry_is = [jnp.where(column == j, 1.0, 0.0).astype(f32) for j in range(8)]

    def listed(ref, window, randoms):
        near_rows = ref[window].reshape(3 * BLOCK, HD)
        return jnp.concatenate([near_rows, ref[g0], ref[g1]] + [ref[r] for r in randoms], axis=0)

    def step(turn, xs, m):
        work = []
        for u in range(UNROLL):
            block = m * UNROLL + u
            n = turn * NBD + block
            i = (xs * SIDE + near) * NBD + block
            bias = entry_is[0] * jnp.where(i == 0, MASKED, 0.0) + entry_is[2] * jnp.where(i == NB - 1, MASKED, 0.0)
            for r in range(R):
                bias = bias + entry_is[5 + r] * off[n * R + r]
            randoms = [named(n * R + r) for r in range(R)]
            work.append((xs * NBD + block, pl.ds(i, 3), randoms, bias, n))
        kc = [listed(ka, t[1], t[2]) for t in work]
        vc = [listed(va, t[1], t[2]) for t in work]
        qn = [qa[t[0]] for t in work]
        dn = [doa[t[0]] for t in work]
        s = [
            lax.dot_general(a, b, NT, preferred_element_type=f32) * scale + t[3]
            for a, b, t in zip(qn, kc, work)
        ]
        dp = [lax.dot_general(a, b, NT, preferred_element_type=f32) for a, b in zip(dn, vc)]
        e = [jnp.exp(a - jnp.max(a, axis=1, keepdims=True)) for a in s]
        p = [a * (1.0 / jnp.sum(a, axis=1, keepdims=True)) for a in e]
        low_p = [a.astype(bf16) for a in p]
        on = [jnp.dot(a, b, preferred_element_type=f32).astype(bf16) for a, b in zip(low_p, vc)]
        delta = [
            jnp.sum(a.astype(f32) * b.astype(f32), axis=1, keepdims=True) for a, b in zip(dn, on)
        ]
        dsc = [(a * (b - d)).astype(bf16) for a, b, d in zip(p, dp, delta)]
        dvt = [lax.dot_general(a, b, TN, preferred_element_type=f32) for a, b in zip(low_p, dn)]
        dkt = [lax.dot_general(a, b, TN, preferred_element_type=f32) for a, b in zip(dsc, qn)]
        dqn = [
            (jnp.dot(a, b, preferred_element_type=f32) * scale).astype(bf16) for a, b in zip(dsc, kc)
        ]
        for t, a, b in zip(work, on, dqn):
            oa[t[0]] = a
            dqa[t[0]] = b
        for total, glob, run, terms in ((dka, dkg, runk, dkt), (dva, dvg, runv, dvt)):
            glob[...] += sum(a[3 * BLOCK : 5 * BLOCK] for a in terms).reshape(G, BLOCK, HD)
            for t, a in zip(work, terms):
                total[t[1]] += a[: 3 * BLOCK].reshape(3, BLOCK, HD)
                for r in range(R):
                    entry = t[4] * R + r
                    run[entry + 1] = a[(5 + r) * BLOCK : (6 + r) * BLOCK] + run[aux[entry]]

    def home_of(xs):
        return {"ctx": xs * SIDE + near, "head": 2 * z + half}

    def source_turn(turn, carry):
        xs = lax.rem(x + turn + 1, SIDE)

        def half_turn(m, inner):
            step(turn, xs, m)
            return inner

        lax.fori_loop(0, NBD // UNROLL, half_turn, 0)
        mine = me & (turn == SIDE - 1)
        for src, dst, send, recv in ((oa, oh, os, orr), (dqa, dqh, gs, gr)):
            copy = remote(src.at[blocks_of(xs)], dst.at[x], send.at[turn], recv.at[x], home_of(xs))
            here = pltpu.make_async_copy(src.at[blocks_of(xs)], dst.at[x], recv.at[x])
            pl.when(jnp.logical_not(mine))(copy.start)
            pl.when(mine)(here.start)
        return carry

    lax.fori_loop(0, SIDE, source_turn, 0)
    for i in range(SIDE):
        xs = lax.rem(x + i + 1, SIDE)
        for src, dst, send, recv in ((oa, oh, os, orr), (dqa, dqh, gs, gr)):
            copy = remote(src.at[blocks_of(xs)], dst.at[x], send.at[i], recv.at[x], home_of(xs))
            if i < SIDE - 1:
                sends.started.append(copy)
            else:
                sends.guarded.append((copy, me))
    for run, glob in ((runk, dkg), (runv, dvg)):
        for i in range(G):
            run[NR + i + 1] = glob[i] + run[aux[NR + i]]
    early.wait()

    def put_sum(ref, j, t, h, total, run, index, factor, also):
        def block(n, carry):
            here = h * CUT + n
            u = index * NBD + here
            value = (total[u + 1] + run[aux[LAST + u]]) * factor
            for other_ref, slot in also:
                value = value + other_ref[slot, t, here].astype(f32)
            ref[j, t, here] = value.astype(bf16)
            return carry

        lax.fori_loop(0, CUT, block, 0)

    totals = ((dka, runk, scale), (dva, runv, 1.0))

    def part(h):
        return pl.ds(h * CUT, CUT)

    def for_other_core(g, there, dx):
        xs = lax.rem(x + dx, SIDE)
        for m, h, t, (total, run, factor) in pieces(*totals):
            put_sum(stage, g + xs, t, h, total, run, xs * SIDE + there, factor, ())
            sends.start(
                remote(stage.at[g + xs, t, part(h)], dcore.at[g + xs, t, part(h)], es.at[g + xs, m], er.at[g + xs, m], other)
            )

    def for_pair(dx):
        xs = lax.rem(x + dx, SIDE)
        for m, h, t, (total, run, factor) in pieces(*totals):
            arrived(dcore.at[xs, t, part(h)], er.at[xs, m])
            put_sum(psend, xs, t, h, total, run, xs * SIDE + pair_near, factor, ((dcore, xs),))
            sends.start(
                remote(psend.at[xs, t, part(h)], dpair.at[xs, t, part(h)], bs.at[xs, m], br.at[xs, m], pair)
            )

    def finish(dx):
        xs = lax.rem(x + dx, SIDE)
        for m, h, t, (total, run, factor) in pieces(*totals):
            arrived(dcore.at[4 + xs, t, part(h)], er.at[4 + xs, m])
            arrived(dpair.at[xs, t, part(h)], br.at[xs, m])
            put_sum(
                nsend, xs, t, h, total, run, xs * SIDE + near, factor, ((dcore, 4 + xs), (dpair, xs))
            )
            src, dst = nsend.at[xs, t, part(h)], (dkh, dvh)[t].at[x, part(h)]
            if dx:
                sends.start(remote(src, dst, hs.at[dx, m], hr.at[x, m], home_of(xs)))
            else:
                sends.start_unless(me, src, dst, hs.at[dx, m], hr.at[x, m], home_of(xs))

    for dx in (2, 1, 3, 0):
        for_other_core(0, other_pair_near, dx)
    for_pair(2)
    for_pair(1)
    for k in range(HPD):
        arrived(oh.at[k], orr.at[k])

    def shard_product(s, put):
        columns = pl.ds(pl.multiple_of(s * SHARD, SHARD), SHARD)

        def tile(i, carry):
            rows = pl.ds(pl.multiple_of(i * PIECE, PIECE), PIECE)
            left = [oh[k, pl.ds(i * CUT, CUT)].reshape(PIECE, HD) for k in range(HPD)]
            left = jnp.concatenate(left, axis=1)
            put(rows, jnp.dot(left, wv[:, columns], preferred_element_type=f32))
            return carry

        lax.fori_loop(0, PIECES, tile, 0)

    for i, s in enumerate((across, above, below, 2 * z)):

        def put(rows, value):
            ogv[i, rows, :] = value.astype(bf16)

        shard_product(s + 1 - c, put)
        sends.start(remote(ogv.at[i], core_in.at[i], c2s.at[i], c2r.at[i], other))

    arrived(core_in.at[0], c2r.at[0])

    def put_across(rows, value):
        ogv[4, rows, :] = (value + core_in[0, rows, :].astype(f32)).astype(bf16)

    shard_product(across + c, put_across)
    for q in range(4):
        sends.start(
            remote(
                ogv.at[4, quarter(q)], hop_in.at[quarter(q)], as_.at[q], ar.at[q], up if q < 2 else down
            )
        )
    for i, s, to in ((0, above, up), (1, below, down)):
        arrived(core_in.at[1 + i], c2r.at[1 + i])

        def put_near(rows, value):
            ogv[5 + i, rows, :] = (value + core_in[1 + i, rows, :].astype(f32)).astype(bf16)

        shard_product(s + c, put_near)
        for q in (2 - 2 * i, 3 - 2 * i):
            sends.start(
                remote(ogv.at[5 + i, quarter(q)], z_in.at[i, quarter(q)], z2s.at[i, q], z2r.at[i, q], to)
            )
    arrived(core_in.at[3], c2r.at[3])

    def put_own(rows, value):
        acc[rows, :] = value + core_in[3, rows, :].astype(f32)

    for_pair(3)
    for_pair(0)
    for dx in (2, 1, 3, 0):
        for_other_core(4, other_near, dx)
    shard_product(hd, put_own)
    for q in range(2):
        for i, to in ((0, up), (1, down)):
            p = q + 2 * i
            arrived(hop_in.at[quarter(p)], ar.at[p])
            ogv[5 + i, quarter(p), :] = (
                ogv[5 + i, quarter(p), :].astype(f32) + hop_in[quarter(p), :].astype(f32)
            ).astype(bf16)
            sends.start(
                remote(ogv.at[5 + i, quarter(p)], z_in.at[i, quarter(p)], z2s.at[i, p], z2r.at[i, p], to)
            )
    for dx in (2, 1, 3, 0):
        finish(dx)
    for i in range(2):
        for q in range(4):
            arrived(z_in.at[i, quarter(q)], z2r.at[i, q])
    proj[...] = (acc[...] + z_in[0].astype(f32) + z_in[1].astype(f32)).astype(bf16)
    for k in range(HPD):
        arrived(dqh.at[k], gr.at[k])
        for m, h, t, out in pieces(dkh, dvh):
            arrived(out.at[k, part(h)], hr.at[k, m])
    sends.wait()


ANY = pl.BlockSpec(memory_space=pl.ANY)
VMEM = pl.BlockSpec(memory_space=pltpu.VMEM)
SMEM = pl.BlockSpec(memory_space=pltpu.SMEM)
LIMIT = 60 * 1024 * 1024


def struct(*shape):
    return jax.ShapeDtypeStruct(shape, jnp.bfloat16)


def sem(*shape):
    return pltpu.SemaphoreType.DMA(shape)


def entries(global_ids, random_ids, random_count):
    _, _, x, y, _, c = place()
    near = query_row(y, c)

    def mine(table):
        rows = lax.dynamic_index_in_dim(table.reshape(SIDE, SIDE, -1), near, 1, keepdims=False)
        return lax.dynamic_slice_in_dim(jnp.concatenate([rows, rows], axis=0), x + 1, SIDE, 0).reshape(-1)

    listed = jnp.concatenate([mine(random_ids), global_ids])
    number = jnp.arange(NR + G, dtype=jnp.int32)
    wanted = jnp.concatenate([listed, jnp.arange(NB, dtype=jnp.int32)])
    limit = jnp.concatenate([number, jnp.full((NB,), NR + G, jnp.int32)])
    hit = (listed[None, :] == wanted[:, None]) & (number[None, :] < limit[:, None])
    chain = jnp.max(jnp.where(hit, number[None, :] + 1, 0), axis=1)
    valid = jnp.arange(R, dtype=jnp.int32)[None, :] < mine(random_count)[:, None]
    return jnp.concatenate([chain, listed + 1]), jnp.where(valid, 0.0, MASKED).astype(jnp.float32).reshape(-1)


def local(queries, key_rows, value_rows, out_weight, out_grad, global_ids, random_ids, random_count):
    bf16, f32 = jnp.bfloat16, jnp.float32
    kvq = jnp.transpose(jnp.stack([key_rows, value_rows, queries], axis=0), (2, 0, 1, 3))
    kvq = kvq.reshape(HPD, 3, NBD, BLOCK, HD)
    w = out_weight.reshape(HPD * HD, out_weight.shape[2])
    both = 2 * PIECES

    def vmem(*shape, dtype=bf16):
        return pltpu.VMEM(shape, dtype)

    def blocks(*count, dtype=bf16):
        return vmem(*count, BLOCK, HD, dtype=dtype)

    one = pltpu.SemaphoreType.DMA
    projected, dqh, dkh, dvh = pl.pallas_call(
        layer_kernel,
        out_shape=(struct(HERE, SHARD),) + (struct(HPD, NBD, BLOCK, HD),) * 3,
        in_specs=[SMEM, SMEM, ANY, ANY, ANY],
        out_specs=(VMEM, ANY, ANY, ANY),
        scratch_shapes=[
            blocks(NB + 2), blocks(NB + 2), blocks(4 * NBD), blocks(4 * NBD), blocks(4 * NBD), blocks(4 * NBD),
            vmem(8, HERE, SHARD), vmem(HERE, SHARD, dtype=f32), blocks(HPD, NBD), vmem(*w.shape),
            blocks(NB + 2, dtype=f32), blocks(NB + 2, dtype=f32), blocks(G, dtype=f32), blocks(G, dtype=f32),
            blocks(NR + G + 1, dtype=f32), blocks(NR + G + 1, dtype=f32),
            blocks(HPD, NBD), vmem(4, HERE, SHARD), vmem(HERE, SHARD), vmem(2, HERE, SHARD),
            blocks(8, 2, NBD), blocks(8, 2, NBD), blocks(4, 2, NBD), blocks(4, 2, NBD), blocks(4, 2, NBD),
            sem(4, both), sem(4, both), sem(4), sem(4), sem(4, both), sem(4, both), sem(8, both), sem(8, both),
            sem(4), sem(4), sem(3, 4), sem(3, 4), sem(4), sem(4), one, one,
            sem(4), sem(4), sem(4), sem(4), sem(8, both), sem(8, both), sem(4, both), sem(4, both),
            sem(4, both), sem(4, both), sem(4), sem(4), sem(4), sem(4), sem(2, 4), sem(2, 4),
        ],
        compiler_params=pltpu.CompilerParams(
            collective_id=0, has_side_effects=True, vmem_limit_bytes=LIMIT
        ),
    )(*entries(global_ids, random_ids, random_count), kvq, out_grad, w)
    grads = [jnp.transpose(g.reshape(HPD, HERE, HD), (1, 0, 2)) for g in (dqh, dkh, dvh)]
    return (projected, *grads)


def solution(mesh):
    placed = (
        P("ctx", "head", None),
        P("ctx", "head", None),
        P("ctx", "head", None),
        P("head", None, None),
        P("ctx", "head"),
        P(),
        P(),
        P(),
    )
    return jax.shard_map(
        local,
        mesh=mesh,
        in_specs=placed,
        out_specs=(
            P("ctx", "head"),
            P("ctx", "head", None),
            P("ctx", "head", None),
            P("ctx", "head", None),
        ),
        check_vma=False,
    )
```

time: 134 us -> 127 us (0.948)
  Pallas kernels: 120 us -> 108 us
  other arithmetic: 1.52 us -> 5.97 us
    pallas_call x3 -> x1, Pallas kernels: 120 us -> 108 us  [local(): pl.pallas_call(layer_kernel, out_shape=(struct(HERE, SHARD),) + (struct(H...]
    unnamed x10 -> x6, local copies, waits for them, and re-layouts: 9.11 us -> 1.63 us
    reshape x1 -> x6, local copies, waits for them, and re-layouts: 0.79 us -> 7.25 us  [the longest x3 6.31 us: local(): g.reshape(HPD, HERE, HD)]
    transpose x0 -> x1, local copies, waits for them, and re-layouts: none -> 1.65 us  [local(): jnp.transpose(jnp.stack([key_rows, value_rows, queries], axis=0), (2, 0,...]
    another operation x1 -> x0, local copies, waits for them, and re-layouts: 1.46 us -> none  [local(): jnp.stack([key_rows, value_rows, queries], axis=0)]
    concatenate x0 -> x4, other arithmetic: none -> 1.41 us  [the longest x1 0.73 us: entries(): wanted = jnp.concatenate([listed, jnp.arange(NB, dtype=jnp.int32)])]
where the time goes in v3:
time: 127 us; the launch traced here: 126 us
  Pallas kernels  108 us (85%)
  local copies, waits for them, and re-layouts  11.3 us (9%)
  other arithmetic  5.97 us (5%)
    pallas_call x1, Pallas kernels, local(): pl.pallas_call(layer_kernel, out_shape=(struct(HERE, SHARD),) + (struct(H...  108 us
    reshape x3, local copies, waits for them, and re-layouts, local(): g.reshape(HPD, HERE, HD)  6.31 us
    transpose x1, other arithmetic, local(): jnp.transpose(jnp.stack([key_rows, value_rows, queries], axis=0), (2, 0,...  2.84 us

profile of v3, /device:TPU:1, one launch (start us, length us, event | category | flops | bytes accessed | tf_op | source)
XLA Modules:
  0.0 126.3 jit_solution(7536595700984102793)
XLA Ops:
  0.7 0.8 reshape.50
  1.5 0.1 lt.46
  1.6 0.1 fusion.1
  1.6 0.6 select_n.32.off
  2.3 0.8 copy.21
  3.1 0.1 reshape.48
  3.2 0.1 reshape.49
  3.3 0.7 pad_add_fusion.2
  4.0 0.7 broadcast_add_fusion
  4.8 0.9 select_reduce_fusion
  5.7 0.7 pad_add_fusion.3.aux
  6.3 2.8 %maximum_bitcast_fusion = bf16[4,3,640,128]{3,0,2,1:T(4,128)(2,1)S(1)} fusion(bf16[1,640,4,128]{3,2,1,0:T(4,128)(2,1)} %bitcast.29, bf16[1,640,4,128]{3,2,1,0:T(4,128)(2,1)} %bitcast.30, bf16[1,640,4,128]{3,2,1,0:T(4,128)(2,1)} %bitcast.31), kind=kLoop, calls=%fused_computation | loop fusion | flops 1966080 | bytes 3932160 | tf_op jit(solution)/shard_map/transpose | solution.py:521
  9.2 1.6 %copy.22 = bf16[4,3,640,128]{3,2,1,0:T(8,128)(2,1)} copy(bf16[4,3,640,128]{3,0,2,1:T(4,128)(2,1)S(1)} %maximum_bitcast_fusion) | data formatting | bytes 3932160 | tf_op jit(solution)/shard_map/transpose | solution.py:521
  10.8 108.3 %shard_map.111 = (bf16[640,512]{1,0:T(8,128)(2,1)}, bf16[4,10,64,128]{3,2,1,0:T(8,128)(2,1)}, bf16[4,10,64,128]{3,2,1,0:T(8,128)(2,1)}, bf16[4,10,64,128]{3,2,1,0:T(8,128)(2,1)}) custom-call(s32[404]{0:T(512)} %pad_add_fusion.3.aux, f32[120]{0:T(128)} %select_n.32.off, bf16[4,3,10,64,128]{4,3,2,1,0:T(8,128)(2,1)} %bitcast.21, bf16[640,512]{1,0:T(8,128)(2,1)} %og.1, ...), custom_call_target="tpu_custom_call" | custom-call | tf_op jit(solution)/shard_map/pallas_call | solution.py:533
  119.1 0.0 copy-start.1
  119.1 0.0 copy-start
  119.1 2.5 %copy.31 = bf16[4,640,128]{2,0,1:T(4,128)(2,1)} copy(bf16[4,640,128]{2,1,0:T(8,128)(2,1)} %bitcast.28) | data formatting | bytes 1310720 | tf_op jit(solution)/shard_map/reshape | solution.py:554
  121.7 2.4 %copy.30 = bf16[4,640,128]{2,0,1:T(4,128)(2,1)} copy(bf16[4,640,128]{2,1,0:T(8,128)(2,1)} %bitcast.27) | data formatting | bytes 1310720 | tf_op jit(solution)/shard_map/reshape | solution.py:554
  124.1 0.0 copy-done.1
  124.1 1.3 %copy.29 = bf16[4,640,128]{2,0,1:T(4,128)(2,1)} copy(bf16[4,640,128]{2,1,0:T(8,128)(2,1)S(1)} %bitcast.26) | data formatting | bytes 1310720 | tf_op jit(solution)/shard_map/reshape | solution.py:554
  125.4 0.0 copy-done
  125.4 0.8 copy.33
  (7 shorter events, 0.1 us)
Async XLA Ops:
  119.1 5.0 %copy-start.1 = (bf16[4,10,64,128]{3,2,1,0:T(8,128)(2,1)S(1)}, bf16[4,10,64,128]{3,2,1,0:T(8,128)(2,1)}, u32[]{:S(2)}) copy-start(bf16[4,10,64,128]{3,2,1,0:T(8,128)(2,1)} %get-tuple-element.11) | copy-start | bytes 1966084
  119.1 6.3 %copy-start = (bf16[640,512]{1,0:T(8,128)(2,1)S(1)}, bf16[640,512]{1,0:T(8,128)(2,1)}, u32[]{:S(2)}) copy-start(bf16[640,512]{1,0:T(8,128)(2,1)} %get-tuple-element.19) | copy-start | bytes 1966084

commit v4 on v3

--- a/solution.py
+++ b/solution.py
@@ -46,7 +46,7 @@
     return pl.ds(index * NBD, NBD)
 
 
-PIECES = 2
+PIECES = 1
 PIECE = HERE // PIECES
 CUT = NBD // PIECES
 
@@ -332,22 +332,20 @@
 
         lax.fori_loop(0, NBD // UNROLL, half_turn, 0)
         mine = me & (turn == SIDE - 1)
-        for src, dst, send, recv in ((oa, oh, os, orr), (dqa, dqh, gs, gr)):
-            copy = remote(src.at[blocks_of(xs)], dst.at[x], send.at[turn], recv.at[x], home_of(xs))
-            here = pltpu.make_async_copy(src.at[blocks_of(xs)], dst.at[x], recv.at[x])
-            pl.when(jnp.logical_not(mine))(copy.start)
-            pl.when(mine)(here.start)
+        copy = remote(oa.at[blocks_of(xs)], oh.at[x], os.at[turn], orr.at[x], home_of(xs))
+        here = pltpu.make_async_copy(oa.at[blocks_of(xs)], oh.at[x], orr.at[x])
+        pl.when(jnp.logical_not(mine))(copy.start)
+        pl.when(mine)(here.start)
         return carry
 
     lax.fori_loop(0, SIDE, source_turn, 0)
     for i in range(SIDE):
         xs = lax.rem(x + i + 1, SIDE)
-        for src, dst, send, recv in ((oa, oh, os, orr), (dqa, dqh, gs, gr)):
-            copy = remote(src.at[blocks_of(xs)], dst.at[x], send.at[i], recv.at[x], home_of(xs))
-            if i < SIDE - 1:
-                sends.started.append(copy)
-            else:
-                sends.guarded.append((copy, me))
+        copy = remote(oa.at[blocks_of(xs)], oh.at[x], os.at[i], orr.at[x], home_of(xs))
+        if i < SIDE - 1:
+            sends.started.append(copy)
+        else:
+            sends.guarded.append((copy, me))
     for run, glob in ((runk, dkg), (runv, dvg)):
         for i in range(G):
             run[NR + i + 1] = glob[i] + run[aux[NR + i]]
@@ -407,6 +405,13 @@
     for_pair(1)
     for k in range(HPD):
         arrived(oh.at[k], orr.at[k])
+    for i in range(SIDE):
+        xs = lax.rem(x + i + 1, SIDE)
+        args = dqa.at[blocks_of(xs)], dqh.at[x], gs.at[i], gr.at[x], home_of(xs)
+        if i < SIDE - 1:
+            sends.start(remote(*args))
+        else:
+            sends.start_unless(me, *args)
 
     def shard_product(s, put):
         columns = pl.ds(pl.multiple_of(s * SHARD, SHARD), SHARD)
@@ -498,28 +503,59 @@
     return pltpu.SemaphoreType.DMA(shape)
 
 
-def entries(global_ids, random_ids, random_count):
+def prepare_kernel(rid, cnt, gid, k, v, q, kvq, aux, off):
     _, _, x, y, _, c = place()
     near = query_row(y, c)
 
-    def mine(table):
-        rows = lax.dynamic_index_in_dim(table.reshape(SIDE, SIDE, -1), near, 1, keepdims=False)
-        return lax.dynamic_slice_in_dim(jnp.concatenate([rows, rows], axis=0), x + 1, SIDE, 0).reshape(-1)
-
-    listed = jnp.concatenate([mine(random_ids), global_ids])
-    number = jnp.arange(NR + G, dtype=jnp.int32)
-    wanted = jnp.concatenate([listed, jnp.arange(NB, dtype=jnp.int32)])
-    limit = jnp.concatenate([number, jnp.full((NB,), NR + G, jnp.int32)])
-    hit = (listed[None, :] == wanted[:, None]) & (number[None, :] < limit[:, None])
-    chain = jnp.max(jnp.where(hit, number[None, :] + 1, 0), axis=1)
-    valid = jnp.arange(R, dtype=jnp.int32)[None, :] < mine(random_count)[:, None]
-    return jnp.concatenate([chain, listed + 1]), jnp.where(valid, 0.0, MASKED).astype(jnp.float32).reshape(-1)
+    def clear(b, carry):
+        aux[LAST + b] = 0
+        return carry
+
+    lax.fori_loop(0, NB, clear, 0, unroll=8)
+
+    def enter_block(entry, block):
+        aux[entry] = aux[LAST + block]
+        aux[LAST + block] = entry + 1
+        aux[LISTED + entry] = block + 1
+
+    for turn in range(SIDE):
+        first = (lax.rem(x + turn + 1, SIDE) * SIDE + near) * NBD
+
+        def query_block(b, carry):
+            i = first + b
+            for r in range(R):
+                entry = (turn * NBD + b) * R + r
+                enter_block(entry, rid[r, i])
+                off[entry] = jnp.where(r < cnt[i], 0.0, MASKED).astype(jnp.float32)
+            if turn < 3:
+                rows = (k, v, q)[turn][pl.ds(b * BLOCK, BLOCK)]
+                kvq[:, turn, b] = jnp.swapaxes(rows, 0, 1)
+            return carry
+
+        lax.fori_loop(0, NBD, query_block, 0)
+    for g in range(G):
+        enter_block(NR + g, gid[g])
+
+
+def finish_kernel(dqh, dkh, dvh, summed, dq, dk, dv, projected):
+    projected[...] = summed[...]
+    for ref, out in ((dqh, dq), (dkh, dk), (dvh, dv)):
+        out[...] = jnp.swapaxes(ref[...].reshape(HPD, HERE, HD), 0, 1)
 
 
 def local(queries, key_rows, value_rows, out_weight, out_grad, global_ids, random_ids, random_count):
     bf16, f32 = jnp.bfloat16, jnp.float32
-    kvq = jnp.transpose(jnp.stack([key_rows, value_rows, queries], axis=0), (2, 0, 1, 3))
-    kvq = kvq.reshape(HPD, 3, NBD, BLOCK, HD)
+    kvq, aux, off = pl.pallas_call(
+        prepare_kernel,
+        out_shape=(
+            struct(HPD, 3, NBD, BLOCK, HD),
+            jax.ShapeDtypeStruct((LISTED + NR + G,), jnp.int32),
+            jax.ShapeDtypeStruct((NR,), jnp.float32),
+        ),
+        in_specs=[SMEM] * 3 + [VMEM] * 3,
+        out_specs=(VMEM, SMEM, SMEM),
+        compiler_params=pltpu.CompilerParams(vmem_limit_bytes=LIMIT),
+    )(random_ids.T, random_count, global_ids, key_rows, value_rows, queries)
     w = out_weight.reshape(HPD * HD, out_weight.shape[2])
     both = 2 * PIECES
 
@@ -530,7 +566,7 @@
         return vmem(*count, BLOCK, HD, dtype=dtype)
 
     one = pltpu.SemaphoreType.DMA
-    projected, dqh, dkh, dvh = pl.pallas_call(
+    summed, dqh, dkh, dvh = pl.pallas_call(
         layer_kernel,
         out_shape=(struct(HERE, SHARD),) + (struct(HPD, NBD, BLOCK, HD),) * 3,
         in_specs=[SMEM, SMEM, ANY, ANY, ANY],
@@ -550,8 +586,14 @@
         compiler_params=pltpu.CompilerParams(
             collective_id=0, has_side_effects=True, vmem_limit_bytes=LIMIT
         ),
-    )(*entries(global_ids, random_ids, random_count), kvq, out_grad, w)
-    grads = [jnp.transpose(g.reshape(HPD, HERE, HD), (1, 0, 2)) for g in (dqh, dkh, dvh)]
+    )(aux, off, kvq, out_grad, w)
+    *grads, projected = pl.pallas_call(
+        finish_kernel,
+        out_shape=(struct(HERE, HPD, HD),) * 3 + (struct(HERE, SHARD),),
+        in_specs=[VMEM] * 4,
+        out_specs=(VMEM,) * 4,
+        compiler_params=pltpu.CompilerParams(vmem_limit_bytes=LIMIT),
+    )(dqh, dkh, dvh, summed)
     return (projected, *grads)
 
 

time: 127 us -> 114 us (0.90)
  local copies, waits for them, and re-layouts: 11.3 us -> 0 us
  other arithmetic: 5.97 us -> 0 us
  Pallas kernels: 108 us -> 113 us
    pallas_call x0 -> x2, Pallas kernels: none -> 8.21 us  [the longest x1 4.95 us: local(): pl.pallas_call(prepare_kernel, out_shape=(struct(HPD, 3, NBD, BLOCK, HD),...]
    reshape x6 -> x0, local copies, waits for them, and re-layouts: 7.25 us -> none  [the longest x3 6.31 us: local(): g.reshape(HPD, HERE, HD)]
    pallas_call x1, Pallas kernels: 108 us -> 105 us  [local(): pl.pallas_call(layer_kernel, out_shape=(struct(HERE, SHARD),) + (struct(H...]
    transpose x1 -> x0, other arithmetic: 2.84 us -> none  [local(): jnp.transpose(jnp.stack([key_rows, value_rows, queries], axis=0), (2, 0,...]
    transpose x1 -> x0, local copies, waits for them, and re-layouts: 1.65 us -> none  [local(): jnp.transpose(jnp.stack([key_rows, value_rows, queries], axis=0), (2, 0,...]
    unnamed x6 -> x0, local copies, waits for them, and re-layouts: 1.63 us -> none
    concatenate x4 -> x0, other arithmetic: 1.41 us -> none  [the longest x1 0.73 us: entries(): wanted = jnp.concatenate([listed, jnp.arange(NB, dtype=jnp.int32)])]
where the time goes in v4:
time: 114 us; the launch traced here: 113 us
  Pallas kernels  113 us (99%)
    pallas_call x1, Pallas kernels, local(): pl.pallas_call(layer_kernel, out_shape=(struct(HERE, SHARD),) + (struct(H...  105 us
    pallas_call x1, Pallas kernels, local(): pl.pallas_call(prepare_kernel, out_shape=(struct(HPD, 3, NBD, BLOCK, HD),...  4.95 us
    pallas_call x1, Pallas kernels, local(): pl.pallas_call(finish_kernel, out_shape=(struct(HERE, HPD, HD),) * 3 + (s...  3.27 us

profile of v4, /device:TPU:1, one launch (start us, length us, event | category | flops | bytes accessed | tf_op | source)
XLA Modules:
  0.0 113.5 jit_solution(13268511707243904806)
XLA Ops:
  0.6 4.9 %shard_map.111 = (bf16[4,3,10,64,128]{4,3,2,1,0:T(8,128)(2,1)}, s32[404]{0:T(512)}, f32[120]{0:T(128)}) custom-call(s32[3,160]{1,0:T(4,128)} %bitcast.3, s32[160]{0:T(256)} %cnt.1, s32[2]{0:T(128)} %gid.1, bf16[640,4,128]{2,1,0:T(4,128)(2,1)} %k.1, bf16[640,4,128]{2,1,0:T(4,128)(2,1)} %v.1, bf16[640,4,128]{2,1,0:T(4,128)(2,1)} %q.1), custom_call_target="tpu_custom_call" | custom-call | tf_op jit(solution)/shard_map/pallas_call | solution.py:548
  5.6 104.6 %shard_map.112 = (bf16[640,512]{1,0:T(8,128)(2,1)}, bf16[4,10,64,128]{3,2,1,0:T(8,128)(2,1)}, bf16[4,10,64,128]{3,2,1,0:T(8,128)(2,1)}, bf16[4,10,64,128]{3,2,1,0:T(8,128)(2,1)}) custom-call(s32[404]{0:T(512)} %get-tuple-element.15.aux, f32[120]{0:T(128)} %get-tuple-element.16.off, bf16[4,3,10,64,128]{4,3,2,1,0:T(8,128)(2,1)} %get-tuple-element.17.kvq, ...), custom_call_target="tpu_custom_call" | custom-call | tf_op jit(solution)/shard_map/pallas_call | solution.py:569
  110.2 3.3 %shard_map.113 = (bf16[640,4,128]{2,1,0:T(4,128)(2,1)}, bf16[640,4,128]{2,1,0:T(4,128)(2,1)}, bf16[640,4,128]{2,1,0:T(4,128)(2,1)}, bf16[640,512]{1,0:T(8,128)(2,1)}) custom-call(bf16[4,10,64,128]{3,2,1,0:T(8,128)(2,1)} %get-tuple-element.18.dqh, bf16[4,10,64,128]{3,2,1,0:T(8,128)(2,1)} %get-tuple-element.19.dkh, ...), custom_call_target="tpu_custom_call" | custom-call | tf_op jit(solution)/shard_map/pallas_call | solution.py:590

commit v5 on v4

--- a/solution.py
+++ b/solution.py
@@ -114,7 +114,7 @@
 
 def layer_kernel(
     aux, off, kvq, og, w, proj, dqh, dkh, dvh,
-    ka, va, qa, doa, oa, dqa, ogv, acc, dov, wv, dka, dva, dkg, dvg, runk, runv,
+    ka, va, qa, doa, oa, dqa, probs, ogv, acc, dov, wv, dka, dva, dkg, dvg, runk, runv,
     oh, core_in, hop_in, z_in, stage, dcore, psend, nsend, dpair,
     ks, kr, qs, qr, ps, pr, fs, fr, ds, dr, zs, zr, cs, cr, own, wsem,
     os, orr, gs, gr, es, er, bs, br, hs, hr, c2s, c2r, as_, ar, z2s, z2r,
@@ -258,7 +258,6 @@
     pass_pair(2)
     for xs in range(SIDE):
         arrived(qa.at[blocks_of(xs)], qr.at[xs])
-        arrived(doa.at[blocks_of(xs)], dr.at[xs])
         for m, h, t, dst in pieces(ka, va):
             arrived(dst.at[padded(xs * SIDE + other_near, h)], fr.at[xs, m])
             arrived(dst.at[padded(xs * SIDE + other_pair_near, h)], fr.at[4 + xs, m])
@@ -276,48 +275,59 @@
         near_rows = ref[window].reshape(3 * BLOCK, HD)
         return jnp.concatenate([near_rows, ref[g0], ref[g1]] + [ref[r] for r in randoms], axis=0)
 
-    def step(turn, xs, m):
-        work = []
+    def work_of(turn, xs, m):
         for u in range(UNROLL):
             block = m * UNROLL + u
             n = turn * NBD + block
             i = (xs * SIDE + near) * NBD + block
+            yield n, xs * NBD + block, i, pl.ds(i, 3), [named(n * R + r) for r in range(R)]
+
+    def forward(turn, xs, m):
+        work, biases = list(work_of(turn, xs, m)), []
+        for n, _, i, _, _ in work:
             bias = entry_is[0] * jnp.where(i == 0, MASKED, 0.0) + entry_is[2] * jnp.where(i == NB - 1, MASKED, 0.0)
             for r in range(R):
                 bias = bias + entry_is[5 + r] * off[n * R + r]
-            randoms = [named(n * R + r) for r in range(R)]
-            work.append((xs * NBD + block, pl.ds(i, 3), randoms, bias, n))
-        kc = [listed(ka, t[1], t[2]) for t in work]
-        vc = [listed(va, t[1], t[2]) for t in work]
-        qn = [qa[t[0]] for t in work]
-        dn = [doa[t[0]] for t in work]
+            biases.append(bias)
+        kc = [listed(ka, t[3], t[4]) for t in work]
+        vc = [listed(va, t[3], t[4]) for t in work]
+        qn = [qa[t[1]] for t in work]
         s = [
-            lax.dot_general(a, b, NT, preferred_element_type=f32) * scale + t[3]
-            for a, b, t in zip(qn, kc, work)
+            lax.dot_general(a, b, NT, preferred_element_type=f32) * scale + bias
+            for a, b, bias in zip(qn, kc, biases)
         ]
+        e = [jnp.exp(a - jnp.max(a, axis=1, keepdims=True)) for a in s]
+        low_p = [(a * (1.0 / jnp.sum(a, axis=1, keepdims=True))).astype(bf16) for a in e]
+        on = [jnp.dot(a, b, preferred_element_type=f32).astype(bf16) for a, b in zip(low_p, vc)]
+        for t, a, b in zip(work, on, low_p):
+            oa[t[1]] = a
+            probs[t[1]] = b
+
+    def backward(turn, xs, m):
+        work = list(work_of(turn, xs, m))
+        kc = [listed(ka, t[3], t[4]) for t in work]
+        vc = [listed(va, t[3], t[4]) for t in work]
+        qn = [qa[t[1]] for t in work]
+        dn = [doa[t[1]] for t in work]
+        low_p = [probs[t[1]] for t in work]
         dp = [lax.dot_general(a, b, NT, preferred_element_type=f32) for a, b in zip(dn, vc)]
-        e = [jnp.exp(a - jnp.max(a, axis=1, keepdims=True)) for a in s]
-        p = [a * (1.0 / jnp.sum(a, axis=1, keepdims=True)) for a in e]
-        low_p = [a.astype(bf16) for a in p]
-        on = [jnp.dot(a, b, preferred_element_type=f32).astype(bf16) for a, b in zip(low_p, vc)]
         delta = [
-            jnp.sum(a.astype(f32) * b.astype(f32), axis=1, keepdims=True) for a, b in zip(dn, on)
+            jnp.sum(a.astype(f32) * oa[t[1]].astype(f32), axis=1, keepdims=True) for a, t in zip(dn, work)
         ]
-        dsc = [(a * (b - d)).astype(bf16) for a, b, d in zip(p, dp, delta)]
+        dsc = [(a.astype(f32) * (b - d)).astype(bf16) for a, b, d in zip(low_p, dp, delta)]
         dvt = [lax.dot_general(a, b, TN, preferred_element_type=f32) for a, b in zip(low_p, dn)]
         dkt = [lax.dot_general(a, b, TN, preferred_element_type=f32) for a, b in zip(dsc, qn)]
         dqn = [
             (jnp.dot(a, b, preferred_element_type=f32) * scale).astype(bf16) for a, b in zip(dsc, kc)
         ]
-        for t, a, b in zip(work, on, dqn):
-            oa[t[0]] = a
-            dqa[t[0]] = b
+        for t, a in zip(work, dqn):
+            dqa[t[1]] = a
         for total, glob, run, terms in ((dka, dkg, runk, dkt), (dva, dvg, runv, dvt)):
             glob[...] += sum(a[3 * BLOCK : 5 * BLOCK] for a in terms).reshape(G, BLOCK, HD)
             for t, a in zip(work, terms):
-                total[t[1]] += a[: 3 * BLOCK].reshape(3, BLOCK, HD)
+                total[t[3]] += a[: 3 * BLOCK].reshape(3, BLOCK, HD)
                 for r in range(R):
-                    entry = t[4] * R + r
+                    entry = t[0] * R + r
                     run[entry + 1] = a[(5 + r) * BLOCK : (6 + r) * BLOCK] + run[aux[entry]]
 
     def home_of(xs):
@@ -327,7 +337,7 @@
         xs = lax.rem(x + turn + 1, SIDE)
 
         def half_turn(m, inner):
-            step(turn, xs, m)
+            forward(turn, xs, m)
             return inner
 
         lax.fori_loop(0, NBD // UNROLL, half_turn, 0)
@@ -339,6 +349,20 @@
         return carry
 
     lax.fori_loop(0, SIDE, source_turn, 0)
+    for xs in range(SIDE):
+        arrived(doa.at[blocks_of(xs)], dr.at[xs])
+
+    def back_turn(turn, carry):
+        xs = lax.rem(x + turn + 1, SIDE)
+
+        def half_turn(m, inner):
+            backward(turn, xs, m)
+            return inner
+
+        lax.fori_loop(0, NBD // UNROLL, half_turn, 0)
+        return carry
+
+    lax.fori_loop(0, SIDE, back_turn, 0)
     for i in range(SIDE):
         xs = lax.rem(x + i + 1, SIDE)
         copy = remote(oa.at[blocks_of(xs)], oh.at[x], os.at[i], orr.at[x], home_of(xs))
@@ -573,6 +597,7 @@
         out_specs=(VMEM, ANY, ANY, ANY),
         scratch_shapes=[
             blocks(NB + 2), blocks(NB + 2), blocks(4 * NBD), blocks(4 * NBD), blocks(4 * NBD), blocks(4 * NBD),
+            vmem(4 * NBD, BLOCK, 8 * BLOCK),
             vmem(8, HERE, SHARD), vmem(HERE, SHARD, dtype=f32), blocks(HPD, NBD), vmem(*w.shape),
             blocks(NB + 2, dtype=f32), blocks(NB + 2, dtype=f32), blocks(G, dtype=f32), blocks(G, dtype=f32),
             blocks(NR + G + 1, dtype=f32), blocks(NR + G + 1, dtype=f32),

time: 114 us -> 107 us (0.939)
  Pallas kernels: 113 us -> 106 us
    pallas_call x1, Pallas kernels: 105 us -> 98 us  [local(): pl.pallas_call(layer_kernel, out_shape=(struct(HERE, SHARD),) + (struct(H...]
where the time goes in v5:
time: 107 us
  Pallas kernels  106 us (99%)
    pallas_call x1, Pallas kernels, local(): pl.pallas_call(layer_kernel, out_shape=(struct(HERE, SHARD),) + (struct(H...  98 us
    pallas_call x1, Pallas kernels, local(): pl.pallas_call(prepare_kernel, out_shape=(struct(HPD, 3, NBD, BLOCK, HD),...  4.95 us
    pallas_call x1, Pallas kernels, local(): pl.pallas_call(finish_kernel, out_shape=(struct(HERE, HPD, HD),) * 3 + (s...  3.27 us

profile of v5, /device:TPU:1, one launch (start us, length us, event | category | flops | bytes accessed | tf_op | source)
XLA Modules:
  0.0 106.9 jit_solution(12935710579510698148)
XLA Ops:
  0.6 4.9 %shard_map.111 = (bf16[4,3,10,64,128]{4,3,2,1,0:T(8,128)(2,1)}, s32[404]{0:T(512)}, f32[120]{0:T(128)}) custom-call(s32[3,160]{1,0:T(4,128)} %bitcast.3, s32[160]{0:T(256)} %cnt.1, s32[2]{0:T(128)} %gid.1, bf16[640,4,128]{2,1,0:T(4,128)(2,1)} %k.1, bf16[640,4,128]{2,1,0:T(4,128)(2,1)} %v.1, bf16[640,4,128]{2,1,0:T(4,128)(2,1)} %q.1), custom_call_target="tpu_custom_call" | custom-call | tf_op jit(solution)/shard_map/pallas_call | solution.py:572
  5.6 98.0 %shard_map.112 = (bf16[640,512]{1,0:T(8,128)(2,1)}, bf16[4,10,64,128]{3,2,1,0:T(8,128)(2,1)}, bf16[4,10,64,128]{3,2,1,0:T(8,128)(2,1)}, bf16[4,10,64,128]{3,2,1,0:T(8,128)(2,1)}) custom-call(s32[404]{0:T(512)} %get-tuple-element.15.aux, f32[120]{0:T(128)} %get-tuple-element.16.off, bf16[4,3,10,64,128]{4,3,2,1,0:T(8,128)(2,1)} %get-tuple-element.17.kvq, ...), custom_call_target="tpu_custom_call" | custom-call | tf_op jit(solution)/shard_map/pallas_call | solution.py:593
  103.6 3.3 %shard_map.113 = (bf16[640,4,128]{2,1,0:T(4,128)(2,1)}, bf16[640,4,128]{2,1,0:T(4,128)(2,1)}, bf16[640,4,128]{2,1,0:T(4,128)(2,1)}, bf16[640,512]{1,0:T(8,128)(2,1)}) custom-call(bf16[4,10,64,128]{3,2,1,0:T(8,128)(2,1)} %get-tuple-element.18.dqh, bf16[4,10,64,128]{3,2,1,0:T(8,128)(2,1)} %get-tuple-element.19.dkh, ...), custom_call_target="tpu_custom_call" | custom-call | tf_op jit(solution)/shard_map/pallas_call | solution.py:615

commit v6 on v5

--- a/solution.py
+++ b/solution.py
@@ -105,7 +105,7 @@
     return pl.ds(q * QUARTER, QUARTER)
 
 
-UNROLL = 5
+UNROLL = 10
 MASKED = -1e30
 NR = 4 * NBD * R
 LAST = NR + G
@@ -535,7 +535,7 @@
         aux[LAST + b] = 0
         return carry
 
-    lax.fori_loop(0, NB, clear, 0, unroll=8)
+    lax.fori_loop(0, NB, clear, 0, unroll=32)
 
     def enter_block(entry, block):
         aux[entry] = aux[LAST + block]
@@ -556,7 +556,7 @@
                 kvq[:, turn, b] = jnp.swapaxes(rows, 0, 1)
             return carry
 
-        lax.fori_loop(0, NBD, query_block, 0)
+        lax.fori_loop(0, NBD, query_block, 0, unroll=5)
     for g in range(G):
         enter_block(NR + g, gid[g])
 

time: 107 us -> 106 us (level)
  no operation moved by 1% of the time
where the time goes in v6:
time: 106 us
  Pallas kernels  105 us (99%)
    pallas_call x1, Pallas kernels, local(): pl.pallas_call(layer_kernel, out_shape=(struct(HERE, SHARD),) + (struct(H...  97.7 us
    pallas_call x1, Pallas kernels, local(): pl.pallas_call(prepare_kernel, out_shape=(struct(HPD, 3, NBD, BLOCK, HD),...  4.34 us
    pallas_call x1, Pallas kernels, local(): pl.pallas_call(finish_kernel, out_shape=(struct(HERE, HPD, HD),) * 3 + (s...  3.27 us

profile of v6, /device:TPU:1, one launch (start us, length us, event | category | flops | bytes accessed | tf_op | source)
XLA Modules:
  0.0 105.9 jit_solution(15595644388670010731)
XLA Ops:
  0.6 4.3 %shard_map.111 = (bf16[4,3,10,64,128]{4,3,2,1,0:T(8,128)(2,1)}, s32[404]{0:T(512)}, f32[120]{0:T(128)}) custom-call(s32[3,160]{1,0:T(4,128)} %bitcast.3, s32[160]{0:T(256)} %cnt.1, s32[2]{0:T(128)} %gid.1, bf16[640,4,128]{2,1,0:T(4,128)(2,1)} %k.1, bf16[640,4,128]{2,1,0:T(4,128)(2,1)} %v.1, bf16[640,4,128]{2,1,0:T(4,128)(2,1)} %q.1), custom_call_target="tpu_custom_call" | custom-call | tf_op jit(solution)/shard_map/pallas_call | solution.py:572
  5.0 97.7 %shard_map.112 = (bf16[640,512]{1,0:T(8,128)(2,1)}, bf16[4,10,64,128]{3,2,1,0:T(8,128)(2,1)}, bf16[4,10,64,128]{3,2,1,0:T(8,128)(2,1)}, bf16[4,10,64,128]{3,2,1,0:T(8,128)(2,1)}) custom-call(s32[404]{0:T(512)} %get-tuple-element.15.aux, f32[120]{0:T(128)} %get-tuple-element.16.off, bf16[4,3,10,64,128]{4,3,2,1,0:T(8,128)(2,1)} %get-tuple-element.17.kvq, ...), custom_call_target="tpu_custom_call" | custom-call | tf_op jit(solution)/shard_map/pallas_call | solution.py:593
  102.7 3.3 %shard_map.113 = (bf16[640,4,128]{2,1,0:T(4,128)(2,1)}, bf16[640,4,128]{2,1,0:T(4,128)(2,1)}, bf16[640,4,128]{2,1,0:T(4,128)(2,1)}, bf16[640,512]{1,0:T(8,128)(2,1)}) custom-call(bf16[4,10,64,128]{3,2,1,0:T(8,128)(2,1)} %get-tuple-element.18.dqh, bf16[4,10,64,128]{3,2,1,0:T(8,128)(2,1)} %get-tuple-element.19.dkh, ...), custom_call_target="tpu_custom_call" | custom-call | tf_op jit(solution)/shard_map/pallas_call | solution.py:615

commit v7 on v6

--- a/solution.py
+++ b/solution.py
@@ -232,20 +232,18 @@
     arrived(ogv.at[2 * z + 1 - c], cr.at[0])
     add_shard(2 * z + 1 - c)
     pass_near((2,))
-    pass_pair(0)
     for i, s in ((0, below), (1, above)):
         for q in range(2):
             p = q + 2 - 2 * i
             arrived(ogv.at[s + c, quarter(p)], zr.at[i, p])
         early.start(remote(ogv.at[s + c], ogv.at[s + c], cs.at[1 + i], cr.at[1 + i], other))
         add_shard(s + c)
+    for p in range(4):
+        arrived(ogv.at[across + c, quarter(p)], zr.at[2, p])
+    early.start(remote(ogv.at[across + c], ogv.at[across + c], cs.at[3], cr.at[3], other))
     for i, s in ((0, below), (1, above)):
         arrived(ogv.at[s + 1 - c], cr.at[1 + i])
         add_shard(s + 1 - c)
-    pass_pair(1)
-    for p in range(4):
-        arrived(ogv.at[across + c, quarter(p)], zr.at[2, p])
-    early.start(remote(ogv.at[across + c], ogv.at[across + c], cs.at[3], cr.at[3], other))
     add_shard(across + c)
     arrived(ogv.at[across + 1 - c], cr.at[3])
     add_shard(across + 1 - c)
@@ -254,6 +252,8 @@
     for dx in (2, 1, 3, 0):
         k = lax.rem(x + dx, SIDE)
         send_worker(dov.at[k], doa.at[blocks_of(x)], ds.at[dx], dr.at[x], dx, k)
+    pass_pair(0)
+    pass_pair(1)
     pass_pair(3)
     pass_pair(2)
     for xs in range(SIDE):

time: 106 us -> 104 us (0.981)
  Pallas kernels: 105 us -> 103 us
    pallas_call x1, Pallas kernels: 97.7 us -> 95.4 us  [local(): pl.pallas_call(layer_kernel, out_shape=(struct(HERE, SHARD),) + (struct(H...]
where the time goes in v7:
time: 104 us
  Pallas kernels  103 us (99%)
    pallas_call x1, Pallas kernels, local(): pl.pallas_call(layer_kernel, out_shape=(struct(HERE, SHARD),) + (struct(H...  95.4 us
    pallas_call x1, Pallas kernels, local(): pl.pallas_call(prepare_kernel, out_shape=(struct(HPD, 3, NBD, BLOCK, HD),...  4.34 us
    pallas_call x1, Pallas kernels, local(): pl.pallas_call(finish_kernel, out_shape=(struct(HERE, HPD, HD),) * 3 + (s...  3.27 us

profile of v7, /device:TPU:1, one launch (start us, length us, event | category | flops | bytes accessed | tf_op | source)
XLA Modules:
  0.0 103.7 jit_solution(5270991830447662445)
XLA Ops:
  0.6 4.3 %shard_map.111 = (bf16[4,3,10,64,128]{4,3,2,1,0:T(8,128)(2,1)}, s32[404]{0:T(512)}, f32[120]{0:T(128)}) custom-call(s32[3,160]{1,0:T(4,128)} %bitcast.3, s32[160]{0:T(256)} %cnt.1, s32[2]{0:T(128)} %gid.1, bf16[640,4,128]{2,1,0:T(4,128)(2,1)} %k.1, bf16[640,4,128]{2,1,0:T(4,128)(2,1)} %v.1, bf16[640,4,128]{2,1,0:T(4,128)(2,1)} %q.1), custom_call_target="tpu_custom_call" | custom-call | tf_op jit(solution)/shard_map/pallas_call | solution.py:572
  5.0 95.4 %shard_map.112 = (bf16[640,512]{1,0:T(8,128)(2,1)}, bf16[4,10,64,128]{3,2,1,0:T(8,128)(2,1)}, bf16[4,10,64,128]{3,2,1,0:T(8,128)(2,1)}, bf16[4,10,64,128]{3,2,1,0:T(8,128)(2,1)}) custom-call(s32[404]{0:T(512)} %get-tuple-element.15.aux, f32[120]{0:T(128)} %get-tuple-element.16.off, bf16[4,3,10,64,128]{4,3,2,1,0:T(8,128)(2,1)} %get-tuple-element.17.kvq, ...), custom_call_target="tpu_custom_call" | custom-call | tf_op jit(solution)/shard_map/pallas_call | solution.py:593
  100.4 3.3 %shard_map.113 = (bf16[640,4,128]{2,1,0:T(4,128)(2,1)}, bf16[640,4,128]{2,1,0:T(4,128)(2,1)}, bf16[640,4,128]{2,1,0:T(4,128)(2,1)}, bf16[640,512]{1,0:T(8,128)(2,1)}) custom-call(bf16[4,10,64,128]{3,2,1,0:T(8,128)(2,1)} %get-tuple-element.18.dqh, bf16[4,10,64,128]{3,2,1,0:T(8,128)(2,1)} %get-tuple-element.19.dkh, ...), custom_call_target="tpu_custom_call" | custom-call | tf_op jit(solution)/shard_map/pallas_call | solution.py:615
